TPU v7x, 128 devices: a whole 4x4x4 slice. The times are simulated.
128 devices in a mesh: row: 16 (over x, z_hi, core), col: 8 (over z_lo, y).
Axes of the slice: x: 4, y: 4, z: 4 (z_hi: 2, z_lo: 2; z = z_hi * 2 + z_lo), core: 2. Of those that a mesh axis runs over, the one named last changes fastest.
Arguments:
- base_weights: bfloat16 [2, 8192, 28672], P(None, 'row', 'col'), may hold values from -6 to 6
- left_factors: bfloat16 [2, 8192, 8, 128], P(None, 'row', 'col'), may hold values from -6 to 6
- right_factors: bfloat16 [2, 8, 128, 28672], P(None, 'col', None, 'row'), may hold values from -6 to 6
- client_adapter_ranks: int32 [8], replicated, may hold values from 16 to 128, as said below
- step_counts: int32 [8], replicated, may hold values from 100 to 1000
- worker_slot: int32 [8], replicated, may hold values from 0 to 7, each once
Outputs:
- merged: bfloat16 [2, 8192, 28672], P(None, 'row', 'col')
Inputs may be any that keep to these rules, and one draw needn't show every extreme that they name: `client_adapter_ranks`: each rank is a multiple of 16; the ranks sum to 512; at least one rank equals 128. `worker_slot`: a permutation: every slot holds exactly one worker's factors.
All inputs are finite; a program needn't handle non-finite values.
Results may differ from a plain program's by a relative error of at most 0.0045.
Values may be sent and summed in bfloat16 or wider, within the bound.
A program may use at most 128 MiB of HBM per device.

v0:
```python
import jax
import jax.numpy as jnp
from jax import lax
from jax.sharding import Mesh
from jax.sharding import PartitionSpec as P

ADAPTER_ALPHA = 32
ROW = ("row_0", "row_1", "row_2")


def sent_to_all(x, axis):
    copies = jnp.broadcast_to(x, (lax.axis_size(axis), *x.shape))
    return lax.all_to_all(copies, axis, split_axis=0, concat_axis=0, tiled=True)


def joined_along(pieces, dim):
    pieces = jnp.moveaxis(pieces, 0, dim)
    shape = pieces.shape
    return pieces.reshape(*shape[:dim], shape[dim] * shape[dim + 1], *shape[dim + 2 :])


def gathered_copies(x, axis, dim):
    pieces = sent_to_all(x, axis)
    return joined_along(pieces, dim)


def gather_in_order(x, axes, order):
    pieces = x[None]
    for k in order:
        pieces = lax.all_gather(pieces, axes[k], axis=0, tiled=True)
    block = [lax.axis_size(axes[k]) for k in reversed(order)]
    pieces = pieces.reshape(*block, *x.shape)
    turned = sorted(range(len(order)), key=lambda place: order[len(order) - 1 - place])
    return pieces.transpose(*turned, *range(len(order), pieces.ndim)).reshape(-1, *x.shape)


def whole_of(x, axes, order, dim):
    return joined_along(gather_in_order(x, axes, order), dim)


def slot_tables(client_adapter_ranks, step_counts, worker_slot):
    workers = client_adapter_ranks.shape[0]
    slot_ids = jnp.arange(workers, dtype=jnp.int32)
    slot_hot = worker_slot[:, None] == slot_ids[None, :]
    rank_slot = jnp.sum(jnp.where(slot_hot, client_adapter_ranks[:, None], 0), axis=0)
    counts = step_counts.astype(jnp.float32)
    per_step_portion = counts / jnp.sum(counts)
    client_scale = ADAPTER_ALPHA * per_step_portion / client_adapter_ranks.astype(jnp.float32)
    slot_scale_factor = jnp.sum(jnp.where(slot_hot, client_scale[:, None], 0.0), axis=0)
    return (rank_slot, slot_scale_factor)


def merge_tile(base_tile, left_piece, right_piece):
    tile_rows = base_tile.shape[0]
    rank_cap = right_piece.shape[1]
    block_width = right_piece.shape[2]
    row_count = lax.axis_size(ROW)
    col_count = lax.axis_size("col")
    row_ratio = row_count // col_count
    left_all = gathered_copies(left_piece, "col", 1)
    sub_width = block_width // row_count
    split_view = right_piece.reshape(1, rank_cap, row_count, sub_width)
    spread = lax.all_to_all(split_view, ROW, split_axis=2, concat_axis=2, tiled=True)
    pair_view = spread.reshape(1, rank_cap, col_count, row_ratio, sub_width)
    slot_pieces = lax.all_to_all(pair_view, "col", split_axis=2, concat_axis=0, tiled=True)
    join_view = slot_pieces.reshape(col_count, rank_cap, row_ratio, 1, sub_width)
    joined = whole_of(join_view, ROW, (1, 0, 2), 3)
    right_cols = joined.reshape(col_count, rank_cap, row_ratio * block_width)
    left_flat = left_all.reshape(tile_rows, -1)
    right_flat = right_cols.reshape(left_flat.shape[1], -1)
    delta_tile = jnp.dot(left_flat, right_flat, preferred_element_type=jnp.float32)
    return (base_tile.astype(jnp.float32) + delta_tile).astype(jnp.bfloat16)


def body(base_weights, left_factors, right_factors, client_adapter_ranks, step_counts, worker_slot):
    workers = client_adapter_ranks.shape[0]
    rank_cap = right_factors.shape[2]
    rank_slot, slot_scale_factor = slot_tables(client_adapter_ranks, step_counts, worker_slot)
    own_hot = jnp.arange(workers, dtype=jnp.int32) == lax.axis_index("col")
    own_rank = jnp.sum(jnp.where(own_hot, rank_slot, 0))
    own_scale = jnp.sum(jnp.where(own_hot, slot_scale_factor, 0.0))
    rank_scale = jnp.where(jnp.arange(rank_cap, dtype=jnp.int32) < own_rank, own_scale, 0.0)
    scaled_right = (right_factors.astype(jnp.float32) * rank_scale[None, None, :, None]).astype(
        jnp.bfloat16
    )
    merged = [
        merge_tile(base_weights[number], left_factors[number], scaled_right[number])
        for number in range(base_weights.shape[0])
    ]
    return jnp.stack(merged)


def solution(mesh):
    finer = Mesh(
        mesh.devices.reshape(4, 2, 2, mesh.shape["col"]), ("row_0", "row_1", "row_2", "col")
    )
    placed = (
        P(None, ROW, "col"),
        P(None, ROW, "col", None),
        P(None, "col", None, ROW),
        P(),
        P(),
        P(),
    )
    return jax.shard_map(
        body, mesh=finer, in_specs=placed, out_specs=P(None, ROW, "col"), check_vma=False
    )
```

profile of v0, /device:TPU:1, one launch (start us, length us, event | category | flops | bytes accessed | tf_op | source)
XLA Modules:
  0.0 256.6 jit_solution(17416153005545980413)
XLA Ops:
  11.9 1.5 copy.49
  15.1 19.5 %all_to_all.50 = bf16[1,128,16,112]{1,3,0,2:T(8,128)(2,1)S(1)} all-to-all(bf16[1,128,16,112]{1,3,0,2:T(8,128)(2,1)S(1)} %bitcast.105), channel_id=1, replica_groups=mesh['row_0'=4,'row_1'=2,'row_2'=2,'col'=8] {'row_0','row_1','row_2'}, dimensions={2} | all-to-all | bytes 917504 | tf_op jit(solution)/shard_map/all_to_all | solution.py:63
  34.6 12.6 %all_to_all.51 = bf16[1,128,8,2,112]{1,4,3,0,2:T(8,128)(2,1)S(1)} all-to-all(bf16[1,128,8,2,112]{1,4,3,0,2:T(8,128)(2,1)S(1)} %bitcast.106), channel_id=1, replica_groups=mesh['row_0'=4,'row_1'=2,'row_2'=2,'col'=8] {'col'}, dimensions={2} | all-to-all | bytes 917504 | tf_op jit(solution)/shard_map/all_to_all | solution.py:65
  47.2 12.0 %all-gather = bf16[16,1,128,1,2,112]{2,5,4,3,1,0:T(8,128)(2,1)} all-gather(bf16[8,1,128,1,2,112]{2,5,4,3,1,0:T(8,128)(2,1)S(1)} %bitcast.108), channel_id=2, replica_groups=mesh['row_0'=4,'row_1'=2,'row_2'=2,'col'=8] {'row_1'}, dimensions={0}, use_global_device_ids=true | all-gather | bytes 1376256 | tf_op jit(solution)/shard_map/all_gather | solution.py:30
  59.3 19.9 %all_to_all.52 = bf16[1,128,16,112]{1,3,0,2:T(8,128)(2,1)S(1)} all-to-all(bf16[1,128,16,112]{1,3,0,2:T(8,128)(2,1)S(1)} %bitcast.104), channel_id=1, replica_groups=mesh['row_0'=4,'row_1'=2,'row_2'=2,'col'=8] {'row_0','row_1','row_2'}, dimensions={2} | all-to-all | bytes 917504 | tf_op jit(solution)/shard_map/all_to_all | solution.py:63
  79.2 11.3 %all_to_all.53 = bf16[1,128,8,2,112]{1,4,3,0,2:T(8,128)(2,1)S(1)} all-to-all(bf16[1,128,8,2,112]{1,4,3,0,2:T(8,128)(2,1)S(1)} %bitcast.107), channel_id=1, replica_groups=mesh['row_0'=4,'row_1'=2,'row_2'=2,'col'=8] {'col'}, dimensions={2} | all-to-all | bytes 917504 | tf_op jit(solution)/shard_map/all_to_all | solution.py:65
  90.4 13.2 %all-gather.1 = bf16[16,1,128,1,2,112]{2,5,4,3,1,0:T(8,128)(2,1)} all-gather(bf16[8,1,128,1,2,112]{2,5,4,3,1,0:T(8,128)(2,1)S(1)} %bitcast.109), channel_id=3, replica_groups=mesh['row_0'=4,'row_1'=2,'row_2'=2,'col'=8] {'row_1'}, dimensions={0}, use_global_device_ids=true | all-gather | bytes 1376256 | tf_op jit(solution)/shard_map/all_gather | solution.py:30
  103.7 2.0 all-gather.7.cloned.1.call-done
  105.8 42.8 %all-gather.11.cloned.1.call-done = bf16[8,8,128,2,1,112]{2,5,4,3,1,0:T(8,128)(2,1)} async-done(((bf16[2,8,128,2,1,112]{2,5,4,3,1,0:T(8,128)(2,1)}), bf16[8,8,128,2,1,112]{2,5,4,3,1,0:T(8,128)(2,1)}) %all-gather.11.cloned.1.call-update) | async-done | bytes 3670032 | tf_op jit(solution)/shard_map/all_gather | solution.py:30
  149.9 5.0 %all-to-all-start.2 = ((bf16[8,512,1,128]{1,3,2,0:T(8,128)(2,1)}), bf16[8,512,1,128]{1,3,2,0:T(8,128)(2,1)S(1)}, u32[]{:S(2)}, u32[]{:S(2)}) async-start(bf16[8,512,1,128]{1,3,2,0:T(8,128)(2,1)} %broadcast_in_dim.59), calls=%async_computation.2 | async-start | bytes 2097152 | tf_op jit(solution)/shard_map/all_to_all | solution.py:13
  154.9 7.4 %fusion.20 = (bf16[1,512,3584]{2,1,0:T(8,128)(2,1)}, bf16[1,512,3584]{2,1,0:T(8,128)(2,1)}) fusion(bf16[2,512,3584]{2,1,0:T(8,128)(2,1)} %param.6), kind=kLoop, calls=%fused_computation.26 | loop fusion | bytes 14680064 | tf_op jit(solution)/shard_map/slice | solution.py:87
  162.2 6.3 %copy.68 = bf16[1,512,3584]{1,2,0:T(8,128)(2,1)} copy(bf16[1,512,3584]{2,1,0:T(8,128)(2,1)} %get-tuple-element.5) | data formatting | bytes 7340032
  168.5 5.9 %copy.69 = bf16[1,512,3584]{1,2,0:T(8,128)(2,1)} copy(bf16[1,512,3584]{2,1,0:T(8,128)(2,1)} %get-tuple-element.6) | data formatting | bytes 7340032
  174.6 4.7 %copy.54 = bf16[4,2,2,8,128,2,1,112]{4,7,6,5,3,2,1,0:T(8,128)(2,1)S(1)} copy(bf16[4,2,2,8,128,2,1,112]{4,7,6,5,3,1,0,2:T(8,128)(2,1)} %bitcast.98) | data formatting | bytes 14680064 | tf_op jit(solution)/shard_map/transpose | solution.py:34
  179.3 6.5 %copy.55 = bf16[8,128,2,16,1,112]{1,0,5,3,2,4:T(8,128)(2,1)} copy(bf16[8,128,2,16,1,112]{1,5,4,2,0,3:T(8,128)(2,1)S(1)} %bitcast.96) | data formatting | bytes 14680064 | tf_op jit(solution)/shard_map/transpose | solution.py:17
  185.8 10.1 %all-gather.13.cloned.1.call-done = bf16[16,8,128,2,1,112]{2,5,4,3,1,0:T(8,128)(2,1)} async-done(((bf16[8,8,128,2,1,112]{2,5,4,3,1,0:T(8,128)(2,1)}), bf16[16,8,128,2,1,112]{2,5,4,3,1,0:T(8,128)(2,1)}) %all-gather.13.cloned.1.call-update) | async-done | bytes 7340048 | tf_op jit(solution)/shard_map/all_gather | solution.py:30
  195.9 4.7 %copy.63 = bf16[4,2,2,8,128,2,1,112]{4,7,6,5,3,2,1,0:T(8,128)(2,1)S(1)} copy(bf16[4,2,2,8,128,2,1,112]{4,7,6,5,3,1,0,2:T(8,128)(2,1)} %bitcast.99) | data formatting | bytes 14680064 | tf_op jit(solution)/shard_map/transpose | solution.py:34
  200.6 5.9 %copy.64 = bf16[8,128,2,16,1,112]{1,0,5,3,2,4:T(8,128)(2,1)} copy(bf16[8,128,2,16,1,112]{1,5,4,2,0,3:T(8,128)(2,1)S(1)} %bitcast.97) | data formatting | bytes 14680064 | tf_op jit(solution)/shard_map/transpose | solution.py:17
  207.5 5.1 %all-to-all-start.5 = ((bf16[8,512,1,128]{1,3,2,0:T(8,128)(2,1)}), bf16[8,512,1,128]{1,3,2,0:T(8,128)(2,1)S(1)}, u32[]{:S(2)}, u32[]{:S(2)}) async-start(bf16[8,512,1,128]{1,3,2,0:T(8,128)(2,1)} %broadcast_in_dim.60), calls=%async_computation.5 | async-start | bytes 2097152 | tf_op jit(solution)/shard_map/all_to_all | solution.py:13
  212.6 9.2 %fusion.12 = bf16[1,512,3584]{1,2,0:T(8,128)(2,1)} fusion(bf16[512,1024]{0,1:T(8,128)(2,1)S(1)} %bitcast.110, bf16[448,8,8,128]{3,2,1,0:T(8,128)(2,1)} %bitcast.100, bf16[1,512,3584]{1,2,0:T(8,128)(2,1)} %copy.68), kind=kOutput, calls=%fused_computation.11 | convolution fusion | flops 3763601408 | bytes 15728640 | tf_op jit(solution)/shard_map/dot_general | solution.py:71
  221.8 6.7 %all-to-all-done.5 = bf16[8,512,1,128]{1,3,2,0:T(8,128)(2,1)S(1)} async-done(((bf16[8,512,1,128]{1,3,2,0:T(8,128)(2,1)}), bf16[8,512,1,128]{1,3,2,0:T(8,128)(2,1)S(1)}, u32[]{:S(2)}, u32[]{:S(2)}) %all-to-all-start.5) | async-done | bytes 1048608 | tf_op jit(solution)/shard_map/all_to_all | solution.py:13
  228.5 8.0 %fusion.15 = bf16[1,512,3584]{1,2,0:T(8,128)(2,1)S(1)} fusion(bf16[512,1024]{0,1:T(8,128)(2,1)S(1)} %bitcast.111, bf16[448,8,8,128]{3,2,1,0:T(8,128)(2,1)} %bitcast.101, bf16[1,512,3584]{1,2,0:T(8,128)(2,1)} %copy.69), kind=kOutput, calls=%fused_computation.12 | convolution fusion | flops 3763601408 | bytes 15728640 | tf_op jit(solution)/shard_map/dot_general | solution.py:71
  236.6 3.6 %pad_maximum_fusion = bf16[2,512,3584]{1,2,0:T(8,128)(2,1)} fusion(bf16[1,512,3584]{1,2,0:T(8,128)(2,1)S(1)} %fusion.15, bf16[1,512,3584]{1,2,0:T(8,128)(2,1)S(1)} %copy-done), kind=kLoop, calls=%fused_computation.6 | loop fusion | flops 3670016 | bytes 14680064 | tf_op jit(solution)/shard_map/stack | solution.py:90
  240.2 9.9 %copy.67 = bf16[2,512,3584]{2,1,0:T(8,128)(2,1)} copy(bf16[2,512,3584]{1,2,0:T(8,128)(2,1)} %pad_maximum_fusion) | data formatting | bytes 14680064 | tf_op jit(solution)/shard_map/stack | solution.py:90
  (28 shorter events, 9.6 us)
Async XLA Ops:
  6.5 99.2 %all-gather.7.cloned.1.call-start = ((), (), s32[]{:S(2)}) async-start(), calls=%async_computation.6 | async-start | bytes 4587520 | tf_op jit(solution)/shard_map/all_gather | solution.py:30
  34.6 114.0 %copy-start.1 = (bf16[2,512,1,128]{3,1,2,0:T(8,128)(2,1)S(1)}, bf16[2,512,1,128]{3,1,2,0:T(8,128)(2,1)}, u32[]{:S(2)}) copy-start(bf16[2,512,1,128]{3,1,2,0:T(8,128)(2,1)} %param.7) | copy-start | bytes 786436
  59.2 89.4 %all-gather.11.cloned.1.call-start = ((), (), s32[]{:S(2)}) async-start(), calls=%async_computation.8 | async-start | bytes 4587520 | tf_op jit(solution)/shard_map/all_gather | solution.py:30
  103.6 70.9 %all-gather.9.cloned.1.call-start = ((), (), s32[]{:S(2)}) async-start(), calls=%async_computation.7 | async-start | bytes 11010048 | tf_op jit(solution)/shard_map/all_gather | solution.py:30
  105.7 90.2 %all-gather.13.cloned.1.call-start = ((), (), s32[]{:S(2)}) async-start(), calls=%async_computation.9 | async-start | bytes 11010048 | tf_op jit(solution)/shard_map/all_gather | solution.py:30
  149.9 56.6 %all-to-all-start.2 = ((bf16[8,512,1,128]{1,3,2,0:T(8,128)(2,1)}), bf16[8,512,1,128]{1,3,2,0:T(8,128)(2,1)S(1)}, u32[]{:S(2)}, u32[]{:S(2)}) async-start(bf16[8,512,1,128]{1,3,2,0:T(8,128)(2,1)} %broadcast_in_dim.59), calls=%async_computation.2 | async-start | bytes 2097152 | tf_op jit(solution)/shard_map/all_to_all | solution.py:13
  207.5 21.0 %all-to-all-start.5 = ((bf16[8,512,1,128]{1,3,2,0:T(8,128)(2,1)}), bf16[8,512,1,128]{1,3,2,0:T(8,128)(2,1)S(1)}, u32[]{:S(2)}, u32[]{:S(2)}) async-start(bf16[8,512,1,128]{1,3,2,0:T(8,128)(2,1)} %broadcast_in_dim.60), calls=%async_computation.5 | async-start | bytes 2097152 | tf_op jit(solution)/shard_map/all_to_all | solution.py:13
  228.5 8.1 %copy-start = (bf16[1,512,3584]{1,2,0:T(8,128)(2,1)S(1)}, bf16[1,512,3584]{1,2,0:T(8,128)(2,1)}, u32[]{:S(2)}) copy-start(bf16[1,512,3584]{1,2,0:T(8,128)(2,1)} %fusion.12) | copy-start | bytes 11010052
Sparse Core Ops, SparseCore 0:
  59.3 46.3 all-gather.6
  107.3 41.1 all-gather.10
  150.2 21.7 all-gather.8
  173.5 22.3 all-gather.12
where the time goes:
time: 258 us; the launch traced here: 257 us
  blocking collectives  88.4 us (34%)
  waiting for transfers between devices  61.6 us (24%)
  local copies, waits for them, and re-layouts  55.3 us (21%)
  matrix products  17.3 us (7%)
  between operations  13.2 us (5%)
  other arithmetic  10.5 us (4%)
  starting transfers between devices  10.2 us (4%)
    all_gather x4, waiting for transfers between devices, gather_in_order(): pieces = lax.all_gather(pieces, axes[k], axis=0, tiled=True)  54.9 us
    all_to_all x2, blocking collectives, merge_tile(): lax.all_to_all(split_view, ROW, split_axis=2, concat_axis=2, tiled=True)  39.4 us
    all_gather x2, blocking collectives, gather_in_order(): pieces = lax.all_gather(pieces, axes[k], axis=0, tiled=True)  25.2 us
    all_to_all x2, blocking collectives, merge_tile(): lax.all_to_all(pair_view, 'col', split_axis=2, concat_axis=0, tiled=True)  23.8 us
    dot_general x2, matrix products, merge_tile(): jnp.dot(left_flat, right_flat, preferred_element_type=jnp.float32)  17.3 us
    unnamed x7, local copies, waits for them, and re-layouts  13.8 us
    transpose x2, local copies, waits for them, and re-layouts, joined_along(): pieces = jnp.moveaxis(pieces, 0, dim)  12.4 us
    all_to_all x2, starting transfers between devices, sent_to_all(): return lax.all_to_all(copies, axis, split_axis=0, concat_axis=0, tiled=True)  10.1 us
  transfers between devices with their start and end apart: 6, of which 4 were waited for; matrix products, arithmetic and copies ran while one was open for 20% of the time, Pallas kernels for 0%

commit v1 on v0

v1 whole, which is shorter than its diff:
```python
import functools

import jax
import jax.numpy as jnp
from jax import lax
from jax.experimental import pallas as pl
from jax.experimental.pallas import tpu as pltpu
from jax.sharding import PartitionSpec as P

ADAPTER_ALPHA = 32
MESH = pl.DeviceIdType.MESH
BF16 = jnp.bfloat16
F32 = jnp.float32
SLOTS = 8
UNIT = 16
ROUTE1_TILES = 9


def slot_ends(ranks, slots):
    ends, total = [], jnp.int32(0)
    for s in range(SLOTS):
        for w in range(SLOTS):
            total = total + jnp.where(slots[w] == s, ranks[w], 0)
        ends.append(total // UNIT)
    return ends


def slot_and_start(position, ends):
    slot = jnp.zeros_like(position)
    start = jnp.zeros_like(position)
    for s in range(SLOTS - 1):
        past = position >= ends[s]
        slot = slot + jnp.where(past, 1, 0)
        start = jnp.where(past, ends[s], start)
    return slot, start


class Copies:
    def __init__(self, send_sems, recv_sems):
        self.send_sems, self.recv_sems = send_sems, recv_sems
        self.count, self.started = 0, []

    def start(self, src, dst, event, device):
        copy = pltpu.make_async_remote_copy(
            src_ref=src,
            dst_ref=dst,
            send_sem=self.send_sems.at[self.count],
            recv_sem=self.recv_sems.at[event],
            device_id=device,
            device_id_type=MESH,
        )
        self.count += 1
        copy.start()
        self.started.append((copy, None))

    def start_or_local(self, src, dst, event, device, local):
        copy = pltpu.make_async_remote_copy(
            src_ref=src,
            dst_ref=dst,
            send_sem=self.send_sems.at[self.count],
            recv_sem=self.recv_sems.at[event],
            device_id=device,
            device_id_type=MESH,
        )
        own = pltpu.make_async_copy(src, dst, self.recv_sems.at[event])
        self.count += 1
        remote = jnp.logical_not(local)
        pl.when(remote)(copy.start)
        pl.when(local)(own.start)
        self.started.append((copy, remote))

    def arrived(self, dst, event, device):
        pltpu.make_async_remote_copy(
            src_ref=dst,
            dst_ref=dst,
            send_sem=self.send_sems.at[0],
            recv_sem=self.recv_sems.at[event],
            device_id=device,
            device_id_type=MESH,
        ).wait_recv()

    def finish(self):
        for copy, when in self.started:
            if when is None:
                copy.wait_send()
            else:
                pl.when(when)(copy.wait_send)


N_A1, N_A2, N_L, N_B = 16, 8, 9, 17 + 16
N_RECV = N_A1 + N_A2 + N_L + 2 * N_B
N_SEND = 16 + 6 + 9 + 2 * 33


def gather_kernel(
    ranks, steps, slots, left, right, r1, r2, packed_left, staged, first, second0, second1, lefts, send_sems, recv_sems
):
    row, col = lax.axis_index("row"), lax.axis_index("col")
    x, zh, core = row // 4, (row // 2) % 2, row % 2
    zl, y = col // 4, col % 4
    t = row // 2

    def dev(x_=x, zh_=zh, core_=core, y_=y, zl_=zl):
        return (x_ * 4 + zh_ * 2 + core_, zl_ * 4 + y_)

    xr, xl, xo = (x + 1) % 4, (x + 3) % 4, (x + 2) % 4
    yr, yl, yo = (y + 1) % 4, (y + 3) % 4, (y + 2) % 4
    zo, co, zlo = 1 - zh, 1 - core, 1 - zl
    right_x, left_x = dev(x_=xr), dev(x_=xl)
    right_y, left_y = dev(y_=yr), dev(y_=yl)
    over_z, sibling, over_zl = dev(zh_=zo), dev(core_=co), dev(zl_=zlo)

    barrier = pltpu.get_barrier_semaphore()
    greeted = [right_x, left_x, over_z, sibling, over_zl, right_y, left_y, dev(y_=yo)]
    for a in range(2):
        for zh0 in range(2):
            for zl0 in range(2):
                greeted.append(dev(x_=2 * zl + a, zh_=zh0, zl_=zl0))
    for device in greeted:
        pl.semaphore_signal(barrier, inc=1, device_id=device, device_id_type=MESH)
    pl.semaphore_wait(barrier, len(greeted))

    copies = Copies(send_sems, recv_sems)
    second = (second0, second1)

    ends = slot_ends(ranks, slots)
    own_rank, own_steps, all_steps = jnp.int32(0), jnp.int32(0), jnp.int32(0)
    for w in range(SLOTS):
        mine = slots[w] == col
        own_rank = own_rank + jnp.where(mine, ranks[w], 0)
        own_steps = own_steps + jnp.where(mine, steps[w], 0)
        all_steps = all_steps + steps[w]
    own_start = jnp.int32(0)
    for s in range(SLOTS - 1):
        own_start = jnp.where(col == s + 1, ends[s], own_start)

    def as_vector(v):
        return jnp.full((1, 128), v, jnp.int32).astype(F32)

    scale = ADAPTER_ALPHA * (as_vector(own_steps) / as_vector(all_steps)) / as_vector(own_rank)
    scale = jnp.concatenate([scale] * (right.shape[3] // 128), axis=1)

    ystar, zlstar = 2 * (x % 2) + zh, x // 2

    def a1_event(p, ystar_, zl_):
        return (p * 4 + ystar_) * 2 + zl_

    for p in range(2):
        for dz in range(2):
            for dx in (2, 1, 3, 0):
                x2, zh2 = (x + dx) % 4, (zh + dz) % 2
                t2 = x2 * 2 + zh2
                k = jnp.bitwise_and(t2 - own_start + 64, 7)
                staged[p, t2] = (right[p, k].astype(F32) * scale).astype(BF16)
                src, dst = staged.at[p, t2], first.at[p, ystar, zl]
                event, device = a1_event(p, ystar, zl), dev(x_=x2, zh_=zh2, zl_=zlstar)
                if dx == 0 and dz == 0:
                    copies.start_or_local(src, dst, event, device, zl == zlstar)
                else:
                    copies.start(src, dst, event, device)
        if p == 0:
            L0 = N_A1 + N_A2
            copies.start(left, lefts.at[col], L0 + 0, right_y)
            copies.start(left, lefts.at[col], L0 + 1, left_y)

    lefts[col] = left[...]

    def a2_event(p, y_):
        return N_A1 + p * 4 + y_

    for p in range(2):
        for dy in (2, 1, 3, 0):
            y2 = (y + dy) % 4
            for zl0 in range(2):
                copies.arrived(first.at[p, y2, zl0], a1_event(p, y2, zl0), sibling)
            if dy:
                copies.start(first.at[p, y2], second[p].at[y], a2_event(p, y), dev(y_=y2))
            else:
                second[p][y] = first[p, y]

    copies.start(left, lefts.at[col], L0 + 2, over_zl)

    def col_of(y_, zl_):
        return zl_ * 4 + y_

    def pass_left(base, zl_):
        c_from_left, c_from_right = col_of(yl, zl_), col_of(yr, zl_)
        copies.arrived(lefts.at[c_from_left], L0 + base, sibling)
        copies.start(lefts.at[c_from_left, 0], lefts.at[c_from_left, 0], L0 + base + 3, right_y)
        copies.arrived(lefts.at[c_from_right], L0 + base + 1, sibling)
        copies.start(lefts.at[c_from_right, 1], lefts.at[c_from_right, 1], L0 + base + 4, left_y)

    pass_left(0, zl)

    BLK = [t, xl * 2 + zh, xr * 2 + zh, xo * 2 + zh, x * 2 + zo, xl * 2 + zo, xr * 2 + zo, xo * 2 + zo]
    HALF = [pl.ds(0, 32), pl.ds(32, 32)]

    def b_event(p, n):
        return N_A1 + N_A2 + N_L + p * N_B + n

    def at(ref, p, blk, rows=None, half=core):
        return ref.at[half, blk, p] if rows is None else ref.at[half, blk, p, rows]

    def go(ref, p, blk, n, device, rows=None):
        copies.start(at(ref, p, blk, rows), at(ref, p, blk, rows), b_event(p, n), device)

    def got(ref, p, blk, n, rows=None, half=core):
        copies.arrived(at(ref, p, blk, rows, half), b_event(p, n), sibling)

    def share(p, route, i):
        go((r1, r2)[route], p, BLK[i], 17 + route * 8 + i, sibling)

    def pack(p):
        for y0 in (1, 2, 3):
            y2 = (y + y0) % 4
            copies.arrived(second[p].at[y2], a2_event(p, y2), sibling)
        width = r1.shape[4]
        for i in range(4):
            slot, _ = slot_and_start(t + 8 * i, ends)
            unit = second[p][jnp.bitwise_and(slot, 3), jnp.right_shift(slot, 2)]
            r1[core, t, p, pl.ds(UNIT * i, UNIT)] = unit[:, :width]
            r2[core, t, p, pl.ds(UNIT * i, UNIT)] = unit[:, width:]
        go(r2, p, t, 0, right_x)
        go(r2, p, t, 1, left_x)
        go(r1, p, t, 8, over_z)
        go(r1, p, t, 9, right_x)
        go(r1, p, t, 10, left_x)
        go(r2, p, t, 4, over_z)
        share(p, 0, 0)
        share(p, 1, 0)

    def early(p):
        got(r2, p, BLK[1], 0)
        go(r2, p, BLK[1], 2, right_x, HALF[0])
        go(r2, p, BLK[1], 5, over_z)
        share(p, 1, 1)
        got(r2, p, BLK[2], 1)
        go(r2, p, BLK[2], 3, left_x, HALF[1])
        go(r2, p, BLK[2], 6, over_z)
        share(p, 1, 2)
        got(r1, p, BLK[4], 8)
        go(r1, p, BLK[4], 13, right_x)
        go(r1, p, BLK[4], 14, left_x)
        share(p, 0, 4)

    def middle(p):
        got(r1, p, BLK[1], 9)
        go(r1, p, BLK[1], 11, right_x, HALF[0])
        share(p, 0, 1)
        got(r1, p, BLK[2], 10)
        go(r1, p, BLK[2], 12, left_x, HALF[1])
        share(p, 0, 2)
        got(r2, p, BLK[3], 2, HALF[0])
        got(r2, p, BLK[3], 3, HALF[1])
        go(r2, p, BLK[3], 7, over_z)
        share(p, 1, 3)
        got(r2, p, BLK[4], 4)
        share(p, 1, 4)

    def late(p):
        got(r1, p, BLK[5], 13)
        go(r1, p, BLK[5], 15, right_x, HALF[0])
        share(p, 0, 5)
        got(r1, p, BLK[6], 14)
        go(r1, p, BLK[6], 16, left_x, HALF[1])
        share(p, 0, 6)
        got(r1, p, BLK[3], 11, HALF[0])
        got(r1, p, BLK[3], 12, HALF[1])
        share(p, 0, 3)
        got(r2, p, BLK[5], 5)
        share(p, 1, 5)
        got(r2, p, BLK[6], 6)
        share(p, 1, 6)

    def last(p):
        got(r2, p, BLK[7], 7)
        share(p, 1, 7)
        got(r1, p, BLK[7], 15, HALF[0])
        got(r1, p, BLK[7], 16, HALF[1])
        share(p, 0, 7)

    def shared(p):
        for route in range(2):
            for i in range(8):
                got((r1, r2)[route], p, BLK[i], 17 + route * 8 + i, half=co)

    pack(0)
    copies.arrived(lefts.at[col_of(y, zlo)], L0 + 2, sibling)
    other = lefts.at[col_of(y, zlo)]
    copies.start(other, other, L0 + 5, right_y)
    copies.start(other, other, L0 + 6, left_y)
    early(0)
    pack(1)
    middle(0)
    early(1)
    c_l, c_r, c_o = col_of(yl, zlo), col_of(yr, zlo), col_of(yo, zlo)
    copies.arrived(lefts.at[c_l], L0 + 5, sibling)
    copies.start(lefts.at[c_l, 0], lefts.at[c_l, 0], L0 + 7, right_y)
    copies.arrived(lefts.at[c_r], L0 + 6, sibling)
    copies.start(lefts.at[c_r, 1], lefts.at[c_r, 1], L0 + 8, left_y)
    late(0)
    middle(1)
    late(1)

    own_o = col_of(yo, zl)
    copies.arrived(lefts.at[own_o, 0], L0 + 3, sibling)
    copies.arrived(lefts.at[own_o, 1], L0 + 4, sibling)
    copies.arrived(lefts.at[c_o, 0], L0 + 7, sibling)
    copies.arrived(lefts.at[c_o, 1], L0 + 8, sibling)
    depth = packed_left.shape[2]
    lane = lax.broadcasted_iota(jnp.int32, (1, depth), 1)
    position = lane // 64 + 8 * ((lane // UNIT) % 4)
    slot, start = slot_and_start(position, ends)
    source = slot * 128 + (position - start) * UNIT + lane % UNIT
    picked = [None, None]
    for s in range(SLOTS):
        k = lax.broadcasted_iota(jnp.int32, (128, depth), 0) + s * 128
        pick = jnp.where(k == source, 1.0, 0.0).astype(BF16)
        for p in range(2):
            part = jnp.dot(lefts[s, p], pick, preferred_element_type=F32)
            picked[p] = part if picked[p] is None else picked[p] + part
    for p in range(2):
        packed_left[p] = picked[p].astype(BF16)

    last(0)
    last(1)
    shared(0)
    shared(1)
    copies.finish()


def merge_kernel(base, packed_left, r1, r2, out):
    width = r1.shape[4]
    lhs = packed_left[0]
    for ref, lo, hi in ((r1, 0, width), (r2, width, out.shape[2])):
        rhs = ref[0, :, 0].reshape(lhs.shape[1], hi - lo)
        delta = jnp.dot(lhs, rhs, preferred_element_type=F32)
        out[0, :, lo:hi] = (base[0, :, lo:hi].astype(F32) + delta).astype(BF16)


def body(base, left, right, ranks, steps, slots):
    projections, rows, columns = base.shape
    half = columns // 2
    left = left.reshape(projections, rows, 128)
    right = right.reshape(projections, 8, UNIT, half)
    w1 = ROUTE1_TILES * 128
    w2 = half - w1
    vmem = pl.BlockSpec(memory_space=pltpu.VMEM)
    smem = pl.BlockSpec(memory_space=pltpu.SMEM)
    r1, r2, packed_left = pl.pallas_call(
        gather_kernel,
        out_shape=(
            jax.ShapeDtypeStruct((2, 8, 2, 64, w1), BF16),
            jax.ShapeDtypeStruct((2, 8, 2, 64, w2), BF16),
            jax.ShapeDtypeStruct((2, rows, 512), BF16),
        ),
        in_specs=[smem, smem, smem, vmem, vmem],
        out_specs=(vmem, vmem, vmem),
        scratch_shapes=[
            pltpu.VMEM((2, 8, UNIT, half), BF16),
            pltpu.VMEM((2, 4, 2, UNIT, half), BF16),
            pltpu.VMEM((4, 2, UNIT, half), BF16),
            pltpu.VMEM((4, 2, UNIT, half), BF16),
            pltpu.VMEM((8, 2, rows, 128), BF16),
            pltpu.SemaphoreType.DMA((N_SEND,)),
            pltpu.SemaphoreType.DMA((N_RECV,)),
        ],
        compiler_params=pltpu.CompilerParams(
            collective_id=0, has_side_effects=True, vmem_limit_bytes=40 * 2**20
        ),
        name="gather_factors",
    )(ranks, steps, slots, left, right)
    return pl.pallas_call(
        merge_kernel,
        grid=(projections, 2),
        out_shape=jax.ShapeDtypeStruct(base.shape, BF16),
        in_specs=[
            pl.BlockSpec((1, rows, half), lambda p, h: (p, 0, h)),
            pl.BlockSpec((1, rows, 512), lambda p, h: (p, 0, 0)),
            pl.BlockSpec((1, 8, 1, 64, w1), lambda p, h: (h, 0, p, 0, 0)),
            pl.BlockSpec((1, 8, 1, 64, w2), lambda p, h: (h, 0, p, 0, 0)),
        ],
        out_specs=pl.BlockSpec((1, rows, half), lambda p, h: (p, 0, h)),
        compiler_params=pltpu.CompilerParams(vmem_limit_bytes=40 * 2**20),
        name="merge_blocks",
    )(base, packed_left, r1, r2)


def solution(mesh):
    placed = (P(None, "row", "col"), P(None, "row", "col", None), P(None, "col", None, "row"), P(), P(), P())
    return jax.shard_map(
        body, mesh=mesh, in_specs=placed, out_specs=P(None, "row", "col"), check_vma=False
    )
```

time: 258 us -> 69.6 us (0.27)
  blocking collectives: 88.4 us -> 0 us
  Pallas kernels: 0 us -> 65.3 us
  waiting for transfers between devices: 61.6 us -> 0 us
  local copies, waits for them, and re-layouts: 55.3 us -> 4.09 us
  matrix products: 17.3 us -> 0 us
  between operations: 13.2 us -> 0.01 us
  other arithmetic: 10.5 us -> 0 us
  starting transfers between devices: 10.2 us -> 0 us
    pallas_call x0 -> x2, Pallas kernels: none -> 65.3 us  [the longest x1 56.2 us: body(): pl.pallas_call(gather_kernel, out_shape=(jax.ShapeDtypeStruct((2, 8, 2, 6...]
    all_to_all x4 -> x0, blocking collectives: 63.3 us -> none  [the longest x2 39.4 us: merge_tile(): lax.all_to_all(split_view, ROW, split_axis=2, concat_axis=2, tiled=True)]
    all_gather x4 -> x0, waiting for transfers between devices: 54.9 us -> none  [gather_in_order(): pieces = lax.all_gather(pieces, axes[k], axis=0, tiled=True)]
    all_gather x2 -> x0, blocking collectives: 25.2 us -> none  [gather_in_order(): pieces = lax.all_gather(pieces, axes[k], axis=0, tiled=True)]
    transpose x4 -> x0, local copies, waits for them, and re-layouts: 21.8 us -> none  [the longest x2 12.4 us: joined_along(): pieces = jnp.moveaxis(pieces, 0, dim)]
    dot_general x2 -> x0, matrix products: 17.3 us -> none  [merge_tile(): jnp.dot(left_flat, right_flat, preferred_element_type=jnp.float32)]
    all_to_all x2 -> x0, starting transfers between devices: 10.1 us -> none  [sent_to_all(): return lax.all_to_all(copies, axis, split_axis=0, concat_axis=0, tiled=True)]
    another operation x1 -> x0, local copies, waits for them, and re-layouts: 9.93 us -> none  [body(): return jnp.stack(merged)]
  transfers between devices with their start and end apart: 6 -> 0, of which waited for: 4 -> 0; matrix products, arithmetic and copies ran while one was open for 20% -> 0% of each run, Pallas kernels for 0% -> 0%
where the time goes in v1:
time: 69.6 us; the launch traced here: 69.4 us
  Pallas kernels  65.3 us (94%)
  local copies, waits for them, and re-layouts  4.09 us (6%)
    pallas_call x1, Pallas kernels, body(): pl.pallas_call(gather_kernel, out_shape=(jax.ShapeDtypeStruct((2, 8, 2, 6...  56.2 us
    pallas_call x1, Pallas kernels, body(): pl.pallas_call(merge_kernel, grid=(projections, 2), out_shape=jax.ShapeDt...  9.07 us
    unnamed x10, local copies, waits for them, and re-layouts  4.09 us

profile of v1, /device:TPU:1, one launch (start us, length us, event | category | flops | bytes accessed | tf_op | source)
XLA Modules:
  0.0 69.4 jit_solution(10016392931035999648)
XLA Ops:
  0.0 0.0 copy-start
  0.0 1.2 %copy-done = bf16[2,1,128,1792]{3,2,1,0:T(8,128)(2,1)S(1)} copy-done((bf16[2,1,128,1792]{3,2,1,0:T(8,128)(2,1)S(1)}, bf16[2,1,128,1792]{3,2,1,0:T(8,128)(2,1)}, u32[]{:S(2)}) %copy-start) | copy-done | bytes 917528
  1.2 0.0 copy-start.1
  1.2 0.9 %copy-done.1 = bf16[2,512,1,128]{3,1,2,0:T(8,128)(2,1)S(1)} copy-done((bf16[2,512,1,128]{3,1,2,0:T(8,128)(2,1)S(1)}, bf16[2,512,1,128]{3,1,2,0:T(8,128)(2,1)}, u32[]{:S(2)}) %copy-start.1) | copy-done | bytes 262168
  2.1 0.0 copy-start.2
  2.1 0.7 copy-done.2
  2.8 0.0 copy-start.3
  2.8 0.7 copy-done.3
  3.4 0.0 copy-start.4
  3.4 0.7 copy-done.4
  4.1 56.2 %gather_factors.1 = (bf16[2,8,2,64,1152]{4,3,2,1,0:T(8,128)(2,1)S(1)}, bf16[2,8,2,64,640]{4,3,2,1,0:T(8,128)(2,1)S(1)}, bf16[2,512,512]{2,1,0:T(8,128)(2,1)S(1)}) custom-call(s32[8]{0:T(128)S(1)} %copy-done.2, s32[8]{0:T(128)S(1)} %copy-done.3, s32[8]{0:T(128)S(1)} %copy-done.4, bf16[2,512,128]{2,1,0:T(8,128)(2,1)S(1)} %bitcast.3, ...), custom_call_target="tpu_custom_call" | custom-call | tf_op jit(solution)/shard_map/gather_factors/pallas_call | solution.py:350
  60.3 9.1 %merge_blocks.1 = bf16[2,512,3584]{2,1,0:T(8,128)(2,1)} custom-call(bf16[2,512,3584]{2,1,0:T(8,128)(2,1)} %base.1, bf16[2,512,512]{2,1,0:T(8,128)(2,1)S(1)} %get-tuple-element.8.packed_left, bf16[2,8,2,64,1152]{4,3,2,1,0:T(8,128)(2,1)S(1)} %get-tuple-element.9.r1, bf16[2,8,2,64,640]{4,3,2,1,0:T(8,128)(2,1)S(1)} %get-tuple-element.10.r2), custom_call_target="tpu_custom_call" | custom-call | tf_op jit(solution)/shard_map/merge_blocks/pallas_call | solution.py:373
Async XLA Ops:
  0.0 1.2 %copy-start = (bf16[2,1,128,1792]{3,2,1,0:T(8,128)(2,1)S(1)}, bf16[2,1,128,1792]{3,2,1,0:T(8,128)(2,1)}, u32[]{:S(2)}) copy-start(bf16[2,1,128,1792]{3,2,1,0:T(8,128)(2,1)} %param.8) | copy-start | bytes 2752516
  1.2 0.9 %copy-start.1 = (bf16[2,512,1,128]{3,1,2,0:T(8,128)(2,1)S(1)}, bf16[2,512,1,128]{3,1,2,0:T(8,128)(2,1)}, u32[]{:S(2)}) copy-start(bf16[2,512,1,128]{3,1,2,0:T(8,128)(2,1)} %param.7) | copy-start | bytes 786436
  2.1 0.7 copy-start.2
  2.8 0.7 copy-start.3
  3.4 0.7 copy-start.4

commit v2 on v1

--- a/solution.py
+++ b/solution.py
@@ -93,7 +93,31 @@
 
 
 def gather_kernel(
-    ranks, steps, slots, left, right, r1, r2, packed_left, staged, first, second0, second1, lefts, send_sems, recv_sems
+    ranks_hbm,
+    steps_hbm,
+    slots_hbm,
+    left,
+    right_hbm,
+    base,
+    r1,
+    r2,
+    packed_left,
+    merged,
+    base_last,
+    ranks,
+    steps,
+    slots,
+    right0,
+    right1,
+    base_first,
+    staged,
+    first,
+    second0,
+    second1,
+    lefts,
+    send_sems,
+    recv_sems,
+    own_sems,
 ):
     row, col = lax.axis_index("row"), lax.axis_index("col")
     x, zh, core = row // 4, (row // 2) % 2, row % 2
@@ -118,10 +142,24 @@
                 greeted.append(dev(x_=2 * zl + a, zh_=zh0, zl_=zl0))
     for device in greeted:
         pl.semaphore_signal(barrier, inc=1, device_id=device, device_id_type=MESH)
-    pl.semaphore_wait(barrier, len(greeted))
 
     copies = Copies(send_sems, recv_sems)
-    second = (second0, second1)
+    second, right = (second0, second1), (right0, right1)
+    pairs = (
+        (ranks_hbm, ranks),
+        (steps_hbm, steps),
+        (slots_hbm, slots),
+        (right_hbm.at[0], right[0]),
+        (right_hbm.at[1], right[1]),
+        (left, lefts.at[col]),
+        (base.at[0], base_first),
+        (base.at[1], base_last),
+    )
+    local = [pltpu.make_async_copy(src, dst, own_sems.at[n]) for n, (src, dst) in enumerate(pairs)]
+    for copy in local[:6]:
+        copy.start()
+    for copy in local[:3]:
+        copy.wait()
 
     ends = slot_ends(ranks, slots)
     own_rank, own_steps, all_steps = jnp.int32(0), jnp.int32(0), jnp.int32(0)
@@ -138,32 +176,57 @@
         return jnp.full((1, 128), v, jnp.int32).astype(F32)
 
     scale = ADAPTER_ALPHA * (as_vector(own_steps) / as_vector(all_steps)) / as_vector(own_rank)
-    scale = jnp.concatenate([scale] * (right.shape[3] // 128), axis=1)
+    scale = jnp.concatenate([scale] * (right0.shape[2] // 128), axis=1)
 
     ystar, zlstar = 2 * (x % 2) + zh, x // 2
 
     def a1_event(p, ystar_, zl_):
         return (p * 4 + ystar_) * 2 + zl_
 
-    for p in range(2):
+    def stage(p):
+        local[3 + p].wait()
+        for t2 in range(8):
+            k = jnp.bitwise_and(t2 - own_start + 64, 7)
+            staged[p, t2] = (right[p][k].astype(F32) * scale).astype(BF16)
+
+    def send_units(p):
         for dz in range(2):
             for dx in (2, 1, 3, 0):
                 x2, zh2 = (x + dx) % 4, (zh + dz) % 2
-                t2 = x2 * 2 + zh2
-                k = jnp.bitwise_and(t2 - own_start + 64, 7)
-                staged[p, t2] = (right[p, k].astype(F32) * scale).astype(BF16)
-                src, dst = staged.at[p, t2], first.at[p, ystar, zl]
+                src, dst = staged.at[p, x2 * 2 + zh2], first.at[p, ystar, zl]
                 event, device = a1_event(p, ystar, zl), dev(x_=x2, zh_=zh2, zl_=zlstar)
                 if dx == 0 and dz == 0:
                     copies.start_or_local(src, dst, event, device, zl == zlstar)
                 else:
                     copies.start(src, dst, event, device)
-        if p == 0:
-            L0 = N_A1 + N_A2
-            copies.start(left, lefts.at[col], L0 + 0, right_y)
-            copies.start(left, lefts.at[col], L0 + 1, left_y)
-
-    lefts[col] = left[...]
+
+    stage(0)
+    pl.semaphore_wait(barrier, len(greeted))
+    send_units(0)
+    stage(1)
+    send_units(1)
+    L0 = N_A1 + N_A2
+    own_left = lefts.at[col]
+    local[5].wait()
+    copies.start(own_left, own_left, L0 + 0, right_y)
+    copies.start(own_left, own_left, L0 + 1, left_y)
+    local[6].start()
+    local[7].start()
+
+    depth = packed_left.shape[2]
+    lane = lax.broadcasted_iota(jnp.int32, (1, depth), 1)
+    position = lane // 64 + 8 * ((lane // UNIT) % 4)
+    lane_slot, lane_start = slot_and_start(position, ends)
+    source = lane_slot * 128 + (position - lane_start) * UNIT + lane % UNIT
+
+    def pick_left(slot, init=False):
+        k = lax.broadcasted_iota(jnp.int32, (128, depth), 0) + slot * 128
+        pick = jnp.where(k == source, 1.0, 0.0).astype(BF16)
+        for p in range(2):
+            part = jnp.dot(lefts[slot, p], pick, preferred_element_type=F32).astype(BF16)
+            packed_left[p] = part if init else packed_left[p] + part
+
+    pick_left(col, init=True)
 
     def a2_event(p, y_):
         return N_A1 + p * 4 + y_
@@ -178,7 +241,7 @@
             else:
                 second[p][y] = first[p, y]
 
-    copies.start(left, lefts.at[col], L0 + 2, over_zl)
+    copies.start(own_left, own_left, L0 + 2, over_zl)
 
     def col_of(y_, zl_):
         return zl_ * 4 + y_
@@ -189,6 +252,8 @@
         copies.start(lefts.at[c_from_left, 0], lefts.at[c_from_left, 0], L0 + base + 3, right_y)
         copies.arrived(lefts.at[c_from_right], L0 + base + 1, sibling)
         copies.start(lefts.at[c_from_right, 1], lefts.at[c_from_right, 1], L0 + base + 4, left_y)
+        pick_left(c_from_left)
+        pick_left(c_from_right)
 
     pass_left(0, zl)
 
@@ -291,6 +356,7 @@
     copies.start(other, other, L0 + 6, left_y)
     early(0)
     pack(1)
+    pick_left(col_of(y, zlo))
     middle(0)
     early(1)
     c_l, c_r, c_o = col_of(yl, zlo), col_of(yr, zlo), col_of(yo, zlo)
@@ -299,43 +365,61 @@
     copies.arrived(lefts.at[c_r], L0 + 6, sibling)
     copies.start(lefts.at[c_r, 1], lefts.at[c_r, 1], L0 + 8, left_y)
     late(0)
-    middle(1)
-    late(1)
-
     own_o = col_of(yo, zl)
     copies.arrived(lefts.at[own_o, 0], L0 + 3, sibling)
     copies.arrived(lefts.at[own_o, 1], L0 + 4, sibling)
+    pick_left(own_o)
+    pick_left(c_l)
+    pick_left(c_r)
+    middle(1)
+    last(0)
+    shared(0)
     copies.arrived(lefts.at[c_o, 0], L0 + 7, sibling)
     copies.arrived(lefts.at[c_o, 1], L0 + 8, sibling)
-    depth = packed_left.shape[2]
-    lane = lax.broadcasted_iota(jnp.int32, (1, depth), 1)
-    position = lane // 64 + 8 * ((lane // UNIT) % 4)
-    slot, start = slot_and_start(position, ends)
-    source = slot * 128 + (position - start) * UNIT + lane % UNIT
-    picked = [None, None]
-    for s in range(SLOTS):
-        k = lax.broadcasted_iota(jnp.int32, (128, depth), 0) + s * 128
-        pick = jnp.where(k == source, 1.0, 0.0).astype(BF16)
-        for p in range(2):
-            part = jnp.dot(lefts[s, p], pick, preferred_element_type=F32)
-            picked[p] = part if picked[p] is None else picked[p] + part
-    for p in range(2):
-        packed_left[p] = picked[p].astype(BF16)
-
-    last(0)
+    pick_left(c_o)
+    late(1)
+    local[6].wait()
+    for h, route, lo, hi in slices(r1.shape[4], r2.shape[4]):
+        merge_slice(0, h, route, lo, hi, base_first, packed_left, r1, r2, merged)
     last(1)
-    shared(0)
     shared(1)
+    local[7].wait()
     copies.finish()
 
 
-def merge_kernel(base, packed_left, r1, r2, out):
-    width = r1.shape[4]
-    lhs = packed_left[0]
-    for ref, lo, hi in ((r1, 0, width), (r2, width, out.shape[2])):
-        rhs = ref[0, :, 0].reshape(lhs.shape[1], hi - lo)
-        delta = jnp.dot(lhs, rhs, preferred_element_type=F32)
-        out[0, :, lo:hi] = (base[0, :, lo:hi].astype(F32) + delta).astype(BF16)
+def slices(width1, width2, step=384):
+    cut = []
+    for h in range(2):
+        for route, width in enumerate((width1, width2)):
+            for lo in range(0, width, step):
+                cut.append((h, route, lo, min(lo + step, width)))
+    return cut
+
+
+def columns_of(h, route, lo, hi, width1, half):
+    start = h * half + route * width1 + lo
+    return slice(start, start + hi - lo)
+
+
+def merge_slice(p, h, route, lo, hi, base, packed_left, r1, r2, out):
+    rhs = (r1, r2)[route][h, :, p, :, lo:hi].reshape(packed_left.shape[2], hi - lo)
+    delta = jnp.dot(packed_left[p], rhs, preferred_element_type=F32)
+    cols = columns_of(h, route, lo, hi, r1.shape[4], base.shape[1] // 2)
+    out[:, cols] = (base[:, cols].astype(F32) + delta).astype(BF16)
+
+
+def merge_kernel(merged, base_last, packed_left, r1, r2, out, last, sems):
+    width1, half = r1.shape[4], base_last.shape[1] // 2
+    started = [pltpu.make_async_copy(merged, out.at[0], sems.at[0])]
+    started[0].start()
+    for n, (h, route, lo, hi) in enumerate(slices(width1, r2.shape[4])):
+        merge_slice(1, h, route, lo, hi, base_last, packed_left, r1, r2, last)
+        cols = columns_of(h, route, lo, hi, width1, half)
+        copy = pltpu.make_async_copy(last.at[:, cols], out.at[1, :, cols], sems.at[n + 1])
+        copy.start()
+        started.append(copy)
+    for copy in started:
+        copy.wait()
 
 
 def body(base, left, right, ranks, steps, slots):
@@ -346,17 +430,25 @@
     w1 = ROUTE1_TILES * 128
     w2 = half - w1
     vmem = pl.BlockSpec(memory_space=pltpu.VMEM)
-    smem = pl.BlockSpec(memory_space=pltpu.SMEM)
-    r1, r2, packed_left = pl.pallas_call(
+    hbm = pl.BlockSpec(memory_space=pltpu.HBM)
+    r1, r2, packed_left, merged, base_last = pl.pallas_call(
         gather_kernel,
         out_shape=(
             jax.ShapeDtypeStruct((2, 8, 2, 64, w1), BF16),
             jax.ShapeDtypeStruct((2, 8, 2, 64, w2), BF16),
             jax.ShapeDtypeStruct((2, rows, 512), BF16),
+            jax.ShapeDtypeStruct((rows, columns), BF16),
+            jax.ShapeDtypeStruct((rows, columns), BF16),
         ),
-        in_specs=[smem, smem, smem, vmem, vmem],
-        out_specs=(vmem, vmem, vmem),
+        in_specs=[hbm] * 6,
+        out_specs=(vmem,) * 5,
         scratch_shapes=[
+            pltpu.SMEM((SLOTS,), jnp.int32),
+            pltpu.SMEM((SLOTS,), jnp.int32),
+            pltpu.SMEM((SLOTS,), jnp.int32),
+            pltpu.VMEM((8, UNIT, half), BF16),
+            pltpu.VMEM((8, UNIT, half), BF16),
+            pltpu.VMEM((rows, columns), BF16),
             pltpu.VMEM((2, 8, UNIT, half), BF16),
             pltpu.VMEM((2, 4, 2, UNIT, half), BF16),
             pltpu.VMEM((4, 2, UNIT, half), BF16),
@@ -364,26 +456,25 @@
             pltpu.VMEM((8, 2, rows, 128), BF16),
             pltpu.SemaphoreType.DMA((N_SEND,)),
             pltpu.SemaphoreType.DMA((N_RECV,)),
+            pltpu.SemaphoreType.DMA((8,)),
         ],
         compiler_params=pltpu.CompilerParams(
-            collective_id=0, has_side_effects=True, vmem_limit_bytes=40 * 2**20
+            collective_id=0, has_side_effects=True, vmem_limit_bytes=32 * 2**20
         ),
         name="gather_factors",
-    )(ranks, steps, slots, left, right)
+    )(*[pltpu.with_memory_space_constraint(a, pltpu.HBM) for a in (ranks, steps, slots, left, right)], base)
     return pl.pallas_call(
         merge_kernel,
-        grid=(projections, 2),
         out_shape=jax.ShapeDtypeStruct(base.shape, BF16),
-        in_specs=[
-            pl.BlockSpec((1, rows, half), lambda p, h: (p, 0, h)),
-            pl.BlockSpec((1, rows, 512), lambda p, h: (p, 0, 0)),
-            pl.BlockSpec((1, 8, 1, 64, w1), lambda p, h: (h, 0, p, 0, 0)),
-            pl.BlockSpec((1, 8, 1, 64, w2), lambda p, h: (h, 0, p, 0, 0)),
+        in_specs=[vmem] * 5,
+        out_specs=pl.BlockSpec(memory_space=pltpu.HBM),
+        scratch_shapes=[
+            pltpu.VMEM((rows, columns), BF16),
+            pltpu.SemaphoreType.DMA((1 + len(slices(w1, w2)),)),
         ],
-        out_specs=pl.BlockSpec((1, rows, half), lambda p, h: (p, 0, h)),
-        compiler_params=pltpu.CompilerParams(vmem_limit_bytes=40 * 2**20),
+        compiler_params=pltpu.CompilerParams(vmem_limit_bytes=24 * 2**20),
         name="merge_blocks",
-    )(base, packed_left, r1, r2)
+    )(merged, base_last, packed_left, r1, r2)
 
 
 def solution(mesh):

time: 69.6 us -> 59.7 us (0.86)
  Pallas kernels: 65.3 us -> 59.6 us
  local copies, waits for them, and re-layouts: 4.09 us -> 0 us
    pallas_call x1, Pallas kernels: 9.07 us -> 3.78 us  [body(): pl.pallas_call(merge_kernel, out_shape=jax.ShapeDtypeStruct(base.shape, B...]
    unnamed x10 -> x0, local copies, waits for them, and re-layouts: 4.09 us -> none
where the time goes in v2:
time: 59.7 us; the launch traced here: 59.6 us
  Pallas kernels  59.6 us (100%)
    pallas_call x1, Pallas kernels, body(): pl.pallas_call(gather_kernel, out_shape=(jax.ShapeDtypeStruct((2, 8, 2, 6...  55.8 us
    pallas_call x1, Pallas kernels, body(): pl.pallas_call(merge_kernel, out_shape=jax.ShapeDtypeStruct(base.shape, B...  3.78 us

profile of v2, /device:TPU:1, one launch (start us, length us, event | category | flops | bytes accessed | tf_op | source)
XLA Modules:
  0.0 59.6 jit_solution(11349129791709437044)
XLA Ops:
  0.0 55.8 %gather_factors.1 = (bf16[2,8,2,64,1152]{4,3,2,1,0:T(8,128)(2,1)S(1)}, bf16[2,8,2,64,640]{4,3,2,1,0:T(8,128)(2,1)S(1)}, bf16[2,512,512]{2,1,0:T(8,128)(2,1)S(1)}...) custom-call(s32[8]{0:T(128)} %ranks_hbm.1, s32[8]{0:T(128)} %steps_hbm.1, s32[8]{0:T(128)} %slots_hbm.1, ...), custom_call_target="tpu_custom_call" | custom-call | tf_op jit(solution)/shard_map/gather_factors/pallas_call | solution.py:434
  55.9 3.8 %merge_blocks.1 = bf16[2,512,3584]{2,1,0:T(8,128)(2,1)} custom-call(bf16[512,3584]{1,0:T(8,128)(2,1)S(1)} %get-tuple-element.10.merged, bf16[512,3584]{1,0:T(8,128)(2,1)S(1)} %get-tuple-element.11.base_last, bf16[2,512,512]{2,1,0:T(8,128)(2,1)S(1)} %get-tuple-element.12.packed_left, bf16[2,8,2,64,1152]{4,3,2,1,0:T(8,128)(2,1)S(1)} %get-tuple-element.13.r1, ...), custom_call_target="tpu_custom_call" | custom-call | tf_op jit(solution)/shard_map/merge_blocks/pallas_call | solution.py:466

commit v3 on v2

--- a/solution.py
+++ b/solution.py
@@ -13,7 +13,16 @@
 F32 = jnp.float32
 SLOTS = 8
 UNIT = 16
+DRAIN = 0
+CHUNKS = 2
 ROUTE1_TILES = 9
+FIRST = (0, 1)
+PACED = {}
+SCHEDULE = (
+    "T0", "L1", "T1", "P0", "L0", "P1", "K0", "E0", "L3", "M0", "L2", "E1", "A0", "K1", "K2",
+    "K4", "M1", "L4", "L5", "K3", "Z0", "A1", "K5", "K6", "L6", "K7", "L7", "H0", "G0", "Z1",
+    "H1",
+)
 
 
 def slot_ends(ranks, slots):
@@ -79,6 +88,14 @@
             device_id_type=MESH,
         ).wait_recv()
 
+    def drain(self, count):
+        for copy, when in self.started[:count]:
+            if when is None:
+                copy.wait_send()
+            else:
+                pl.when(when)(copy.wait_send)
+        self.started = self.started[count:]
+
     def finish(self):
         for copy, when in self.started:
             if when is None:
@@ -87,9 +104,9 @@
                 pl.when(when)(copy.wait_send)
 
 
-N_A1, N_A2, N_L, N_B = 16, 8, 9, 17 + 16
-N_RECV = N_A1 + N_A2 + N_L + 2 * N_B
-N_SEND = 16 + 6 + 9 + 2 * 33
+N_A1, N_A2, N_L, N_B = CHUNKS * 8, CHUNKS * 4, 9, 17 + 16
+N_RECV = N_A1 + N_A2 + N_L + CHUNKS * N_B
+N_SEND = CHUNKS * (8 + 3 + N_B) + 9
 
 
 def gather_kernel(
@@ -102,23 +119,17 @@
     r1,
     r2,
     packed_left,
-    merged,
-    base_last,
+    work,
     ranks,
     steps,
     slots,
     right0,
     right1,
-    base_first,
     staged,
     first,
-    second0,
-    second1,
-    lefts,
-    send_sems,
-    recv_sems,
-    own_sems,
+    *rest,
 ):
+    second, (lefts, send_sems, recv_sems, own_sems) = rest[:CHUNKS], rest[CHUNKS:]
     row, col = lax.axis_index("row"), lax.axis_index("col")
     x, zh, core = row // 4, (row // 2) % 2, row % 2
     zl, y = col // 4, col % 4
@@ -144,7 +155,8 @@
         pl.semaphore_signal(barrier, inc=1, device_id=device, device_id_type=MESH)
 
     copies = Copies(send_sems, recv_sems)
-    second, right = (second0, second1), (right0, right1)
+    right = (right0, right1)
+    chunk_width = staged.shape[3]
     pairs = (
         (ranks_hbm, ranks),
         (steps_hbm, steps),
@@ -152,8 +164,8 @@
         (right_hbm.at[0], right[0]),
         (right_hbm.at[1], right[1]),
         (left, lefts.at[col]),
-        (base.at[0], base_first),
-        (base.at[1], base_last),
+        (base.at[0], work.at[0]),
+        (base.at[1], work.at[1]),
     )
     local = [pltpu.make_async_copy(src, dst, own_sems.at[n]) for n, (src, dst) in enumerate(pairs)]
     for copy in local[:6]:
@@ -176,40 +188,49 @@
         return jnp.full((1, 128), v, jnp.int32).astype(F32)
 
     scale = ADAPTER_ALPHA * (as_vector(own_steps) / as_vector(all_steps)) / as_vector(own_rank)
-    scale = jnp.concatenate([scale] * (right0.shape[2] // 128), axis=1)
+    scale = jnp.concatenate([scale] * (chunk_width // 128), axis=1)
 
     ystar, zlstar = 2 * (x % 2) + zh, x // 2
 
     def a1_event(p, ystar_, zl_):
         return (p * 4 + ystar_) * 2 + zl_
 
-    def stage(p):
-        local[3 + p].wait()
+    def stage(c):
+        p, lo = place(c, chunk_width)
+        if lo == 0:
+            local[3 + p].wait()
         for t2 in range(8):
             k = jnp.bitwise_and(t2 - own_start + 64, 7)
-            staged[p, t2] = (right[p][k].astype(F32) * scale).astype(BF16)
-
-    def send_units(p):
-        for dz in range(2):
-            for dx in (2, 1, 3, 0):
-                x2, zh2 = (x + dx) % 4, (zh + dz) % 2
-                src, dst = staged.at[p, x2 * 2 + zh2], first.at[p, ystar, zl]
-                event, device = a1_event(p, ystar, zl), dev(x_=x2, zh_=zh2, zl_=zlstar)
-                if dx == 0 and dz == 0:
-                    copies.start_or_local(src, dst, event, device, zl == zlstar)
-                else:
-                    copies.start(src, dst, event, device)
+            staged[c, t2] = (right[p][k][:, lo : lo + chunk_width].astype(F32) * scale).astype(BF16)
+
+    def send_unit(c, n):
+        dx, dz = (2, 1, 3, 0)[n % 4], n // 4
+        x2, zh2 = (x + dx) % 4, (zh + dz) % 2
+        src, dst = staged.at[c, x2 * 2 + zh2], first.at[c, ystar, zl]
+        event, device = a1_event(c, ystar, zl), dev(x_=x2, zh_=zh2, zl_=zlstar)
+        if dx == 0 and dz == 0:
+            copies.start_or_local(src, dst, event, device, zl == zlstar)
+        else:
+            copies.start(src, dst, event, device)
 
     stage(0)
     pl.semaphore_wait(barrier, len(greeted))
-    send_units(0)
-    stage(1)
-    send_units(1)
+
+    def send_units(c):
+        if c:
+            stage(c)
+            copies.drain(DRAIN)
+        for n in range(8):
+            send_unit(c, n)
+
+    for c in FIRST:
+        send_units(c)
+    for c in range(CHUNKS):
+        if c not in FIRST:
+            stage(c)
     L0 = N_A1 + N_A2
     own_left = lefts.at[col]
     local[5].wait()
-    copies.start(own_left, own_left, L0 + 0, right_y)
-    copies.start(own_left, own_left, L0 + 1, left_y)
     local[6].start()
     local[7].start()
 
@@ -231,17 +252,18 @@
     def a2_event(p, y_):
         return N_A1 + p * 4 + y_
 
-    for p in range(2):
-        for dy in (2, 1, 3, 0):
+    def turn(c):
+        for n, dy in enumerate((2, 1, 3, 0)):
             y2 = (y + dy) % 4
             for zl0 in range(2):
-                copies.arrived(first.at[p, y2, zl0], a1_event(p, y2, zl0), sibling)
+                copies.arrived(first.at[c, y2, zl0], a1_event(c, y2, zl0), sibling)
             if dy:
-                copies.start(first.at[p, y2], second[p].at[y], a2_event(p, y), dev(y_=y2))
+                copies.start(first.at[c, y2], second[c].at[y], a2_event(c, y), dev(y_=y2))
             else:
-                second[p][y] = first[p, y]
-
-    copies.start(own_left, own_left, L0 + 2, over_zl)
+                second[c][y] = first[c, y]
+            if c in PACED:
+                send_unit(PACED[c], 2 * n)
+                send_unit(PACED[c], 2 * n + 1)
 
     def col_of(y_, zl_):
         return zl_ * 4 + y_
@@ -252,10 +274,7 @@
         copies.start(lefts.at[c_from_left, 0], lefts.at[c_from_left, 0], L0 + base + 3, right_y)
         copies.arrived(lefts.at[c_from_right], L0 + base + 1, sibling)
         copies.start(lefts.at[c_from_right, 1], lefts.at[c_from_right, 1], L0 + base + 4, left_y)
-        pick_left(c_from_left)
-        pick_left(c_from_right)
-
-    pass_left(0, zl)
+
 
     BLK = [t, xl * 2 + zh, xr * 2 + zh, xo * 2 + zh, x * 2 + zo, xl * 2 + zo, xr * 2 + zo, xo * 2 + zo]
     HALF = [pl.ds(0, 32), pl.ds(32, 32)]
@@ -264,7 +283,7 @@
         return N_A1 + N_A2 + N_L + p * N_B + n
 
     def at(ref, p, blk, rows=None, half=core):
-        return ref.at[half, blk, p] if rows is None else ref.at[half, blk, p, rows]
+        return ref.at[p, half, blk] if rows is None else ref.at[p, half, blk, rows]
 
     def go(ref, p, blk, n, device, rows=None):
         copies.start(at(ref, p, blk, rows), at(ref, p, blk, rows), b_event(p, n), device)
@@ -283,8 +302,8 @@
         for i in range(4):
             slot, _ = slot_and_start(t + 8 * i, ends)
             unit = second[p][jnp.bitwise_and(slot, 3), jnp.right_shift(slot, 2)]
-            r1[core, t, p, pl.ds(UNIT * i, UNIT)] = unit[:, :width]
-            r2[core, t, p, pl.ds(UNIT * i, UNIT)] = unit[:, width:]
+            r1[p, core, t, pl.ds(UNIT * i, UNIT)] = unit[:, :width]
+            r2[p, core, t, pl.ds(UNIT * i, UNIT)] = unit[:, width:]
         go(r2, p, t, 0, right_x)
         go(r2, p, t, 1, left_x)
         go(r1, p, t, 8, over_z)
@@ -349,45 +368,67 @@
             for i in range(8):
                 got((r1, r2)[route], p, BLK[i], 17 + route * 8 + i, half=co)
 
-    pack(0)
-    copies.arrived(lefts.at[col_of(y, zlo)], L0 + 2, sibling)
-    other = lefts.at[col_of(y, zlo)]
-    copies.start(other, other, L0 + 5, right_y)
-    copies.start(other, other, L0 + 6, left_y)
-    early(0)
-    pack(1)
-    pick_left(col_of(y, zlo))
-    middle(0)
-    early(1)
-    c_l, c_r, c_o = col_of(yl, zlo), col_of(yr, zlo), col_of(yo, zlo)
-    copies.arrived(lefts.at[c_l], L0 + 5, sibling)
-    copies.start(lefts.at[c_l, 0], lefts.at[c_l, 0], L0 + 7, right_y)
-    copies.arrived(lefts.at[c_r], L0 + 6, sibling)
-    copies.start(lefts.at[c_r, 1], lefts.at[c_r, 1], L0 + 8, left_y)
-    late(0)
-    own_o = col_of(yo, zl)
-    copies.arrived(lefts.at[own_o, 0], L0 + 3, sibling)
-    copies.arrived(lefts.at[own_o, 1], L0 + 4, sibling)
-    pick_left(own_o)
-    pick_left(c_l)
-    pick_left(c_r)
-    middle(1)
-    last(0)
-    shared(0)
-    copies.arrived(lefts.at[c_o, 0], L0 + 7, sibling)
-    copies.arrived(lefts.at[c_o, 1], L0 + 8, sibling)
-    pick_left(c_o)
-    late(1)
-    local[6].wait()
-    for h, route, lo, hi in slices(r1.shape[4], r2.shape[4]):
-        merge_slice(0, h, route, lo, hi, base_first, packed_left, r1, r2, merged)
-    last(1)
-    shared(1)
-    local[7].wait()
+    def start_left():
+        copies.start(own_left, own_left, L0 + 0, right_y)
+        copies.start(own_left, own_left, L0 + 1, left_y)
+
+    def cross_left():
+        other = lefts.at[col_of(y, zlo)]
+        copies.arrived(other, L0 + 2, sibling)
+        copies.start(other, other, L0 + 5, right_y)
+        copies.start(other, other, L0 + 6, left_y)
+
+    c_l, c_r, c_o, own_o = col_of(yl, zlo), col_of(yr, zlo), col_of(yo, zlo), col_of(yo, zl)
+
+    def pass_other_left():
+        copies.arrived(lefts.at[c_l], L0 + 5, sibling)
+        copies.start(lefts.at[c_l, 0], lefts.at[c_l, 0], L0 + 7, right_y)
+        copies.arrived(lefts.at[c_r], L0 + 6, sibling)
+        copies.start(lefts.at[c_r, 1], lefts.at[c_r, 1], L0 + 8, left_y)
+
+    def merge(c):
+        for h, route, lo, hi in slices(r1.shape[4], r2.shape[4]):
+            merge_slice(c, h, route, lo, hi, work, packed_left, r1, r2)
+
+    def own_halves():
+        copies.arrived(lefts.at[own_o, 0], L0 + 3, sibling)
+        copies.arrived(lefts.at[own_o, 1], L0 + 4, sibling)
+
+    def other_halves():
+        copies.arrived(lefts.at[c_o, 0], L0 + 7, sibling)
+        copies.arrived(lefts.at[c_o, 1], L0 + 8, sibling)
+
+    def load_base():
+        local[6].wait()
+        local[7].wait()
+
+    steps_of = {
+        "T": turn, "P": pack, "E": early, "M": middle, "A": late, "Z": last, "H": shared, "G": merge,
+        "L": lambda n: (
+            start_left,
+            lambda: copies.start(own_left, own_left, L0 + 2, over_zl),
+            lambda: pass_left(0, zl),
+            cross_left,
+            pass_other_left,
+            own_halves,
+            other_halves,
+            load_base,
+        )[n](),
+        "K": lambda n: pick_left(
+            (col, col_of(yl, zl), col_of(yr, zl), own_o, col_of(y, zlo), c_l, c_r, c_o)[n], init=n == 0
+        ),
+    }
+    for step in SCHEDULE:
+        steps_of[step[0]](int(step[1]))
     copies.finish()
 
 
-def slices(width1, width2, step=384):
+def place(chunk, width):
+    per = CHUNKS // 2
+    return chunk // per, (chunk % per) * width
+
+
+def slices(width1, width2, step=512):
     cut = []
     for h in range(2):
         for route, width in enumerate((width1, width2)):
@@ -396,28 +437,40 @@
     return cut
 
 
-def columns_of(h, route, lo, hi, width1, half):
-    start = h * half + route * width1 + lo
-    return slice(start, start + hi - lo)
-
-
-def merge_slice(p, h, route, lo, hi, base, packed_left, r1, r2, out):
-    rhs = (r1, r2)[route][h, :, p, :, lo:hi].reshape(packed_left.shape[2], hi - lo)
+def merge_slice(c, h, route, lo, hi, work, packed_left, r1, r2, out=None):
+    width1, half = r1.shape[4], work.shape[2] // 2
+    p, first = place(c, width1 + r2.shape[4])
+    begin = h * half + first + route * width1 + lo
+    cols = slice(begin, begin + hi - lo)
+    rhs = (r1, r2)[route][c, h, :, :, lo:hi].reshape(packed_left.shape[2], hi - lo)
     delta = jnp.dot(packed_left[p], rhs, preferred_element_type=F32)
-    cols = columns_of(h, route, lo, hi, r1.shape[4], base.shape[1] // 2)
-    out[:, cols] = (base[:, cols].astype(F32) + delta).astype(BF16)
-
-
-def merge_kernel(merged, base_last, packed_left, r1, r2, out, last, sems):
-    width1, half = r1.shape[4], base_last.shape[1] // 2
-    started = [pltpu.make_async_copy(merged, out.at[0], sems.at[0])]
-    started[0].start()
-    for n, (h, route, lo, hi) in enumerate(slices(width1, r2.shape[4])):
-        merge_slice(1, h, route, lo, hi, base_last, packed_left, r1, r2, last)
-        cols = columns_of(h, route, lo, hi, width1, half)
-        copy = pltpu.make_async_copy(last.at[:, cols], out.at[1, :, cols], sems.at[n + 1])
+    total = (work[p, :, cols].astype(F32) + delta).astype(BF16)
+    if out is None:
+        work[p, :, cols] = total
+    else:
+        out[:, cols] = total
+    return p, cols
+
+
+def merge_kernel(work, packed_left, r1, r2, out, last, sems):
+    width1, width2, half = r1.shape[4], r2.shape[4], work.shape[2] // 2
+    p, lo = place(CHUNKS - 1, width1 + width2)
+    pairs = [(work.at[p2], out.at[p2]) for p2 in range(p)]
+    for h in range(2 if lo else 0):
+        cols = slice(h * half, h * half + lo)
+        pairs.append((work.at[p, :, cols], out.at[p, :, cols]))
+    started = []
+
+    def send(src, dst):
+        copy = pltpu.make_async_copy(src, dst, sems.at[len(started)])
         copy.start()
         started.append(copy)
+
+    for src, dst in pairs:
+        send(src, dst)
+    for h, route, lo, hi in slices(width1, width2):
+        p, cols = merge_slice(CHUNKS - 1, h, route, lo, hi, work, packed_left, r1, r2, last)
+        send(last.at[:, cols], out.at[p, :, cols])
     for copy in started:
         copy.wait()
 
@@ -427,54 +480,49 @@
     half = columns // 2
     left = left.reshape(projections, rows, 128)
     right = right.reshape(projections, 8, UNIT, half)
+    width = 2 * half // CHUNKS
     w1 = ROUTE1_TILES * 128
-    w2 = half - w1
+    w2 = width - w1
     vmem = pl.BlockSpec(memory_space=pltpu.VMEM)
     hbm = pl.BlockSpec(memory_space=pltpu.HBM)
-    r1, r2, packed_left, merged, base_last = pl.pallas_call(
+    r1, r2, packed_left, work = pl.pallas_call(
         gather_kernel,
         out_shape=(
-            jax.ShapeDtypeStruct((2, 8, 2, 64, w1), BF16),
-            jax.ShapeDtypeStruct((2, 8, 2, 64, w2), BF16),
+            jax.ShapeDtypeStruct((CHUNKS, 2, 8, 64, w1), BF16),
+            jax.ShapeDtypeStruct((CHUNKS, 2, 8, 64, w2), BF16),
             jax.ShapeDtypeStruct((2, rows, 512), BF16),
-            jax.ShapeDtypeStruct((rows, columns), BF16),
-            jax.ShapeDtypeStruct((rows, columns), BF16),
+            jax.ShapeDtypeStruct(base.shape, BF16),
         ),
         in_specs=[hbm] * 6,
-        out_specs=(vmem,) * 5,
+        out_specs=(vmem,) * 4,
         scratch_shapes=[
             pltpu.SMEM((SLOTS,), jnp.int32),
             pltpu.SMEM((SLOTS,), jnp.int32),
             pltpu.SMEM((SLOTS,), jnp.int32),
             pltpu.VMEM((8, UNIT, half), BF16),
             pltpu.VMEM((8, UNIT, half), BF16),
-            pltpu.VMEM((rows, columns), BF16),
-            pltpu.VMEM((2, 8, UNIT, half), BF16),
-            pltpu.VMEM((2, 4, 2, UNIT, half), BF16),
-            pltpu.VMEM((4, 2, UNIT, half), BF16),
-            pltpu.VMEM((4, 2, UNIT, half), BF16),
+            pltpu.VMEM((CHUNKS, 8, UNIT, width), BF16),
+            pltpu.VMEM((CHUNKS, 4, 2, UNIT, width), BF16),
+            *[pltpu.VMEM((4, 2, UNIT, width), BF16)] * CHUNKS,
             pltpu.VMEM((8, 2, rows, 128), BF16),
             pltpu.SemaphoreType.DMA((N_SEND,)),
             pltpu.SemaphoreType.DMA((N_RECV,)),
             pltpu.SemaphoreType.DMA((8,)),
         ],
         compiler_params=pltpu.CompilerParams(
-            collective_id=0, has_side_effects=True, vmem_limit_bytes=32 * 2**20
+            collective_id=0, has_side_effects=True, vmem_limit_bytes=24 * 2**20
         ),
         name="gather_factors",
-    )(*[pltpu.with_memory_space_constraint(a, pltpu.HBM) for a in (ranks, steps, slots, left, right)], base)
+    )(*[pltpu.with_memory_space_constraint(a, pltpu.HBM) for a in (ranks, steps, slots, left, right, base)])
     return pl.pallas_call(
         merge_kernel,
         out_shape=jax.ShapeDtypeStruct(base.shape, BF16),
-        in_specs=[vmem] * 5,
+        in_specs=[vmem] * 4,
         out_specs=pl.BlockSpec(memory_space=pltpu.HBM),
-        scratch_shapes=[
-            pltpu.VMEM((rows, columns), BF16),
-            pltpu.SemaphoreType.DMA((1 + len(slices(w1, w2)),)),
-        ],
+        scratch_shapes=[pltpu.VMEM((rows, columns), BF16), pltpu.SemaphoreType.DMA((16,))],
         compiler_params=pltpu.CompilerParams(vmem_limit_bytes=24 * 2**20),
         name="merge_blocks",
-    )(merged, base_last, packed_left, r1, r2)
+    )(work, packed_left, r1, r2)
 
 
 def solution(mesh):

time: 59.7 us -> 57.5 us (0.963)
  Pallas kernels: 59.6 us -> 57.4 us
    pallas_call x1, Pallas kernels: 55.8 us -> 54.2 us  [body(): pl.pallas_call(gather_kernel, out_shape=(jax.ShapeDtypeStruct((CHUNKS, 2,...]
    pallas_call x1, Pallas kernels: 3.78 us -> 3.17 us  [body(): pl.pallas_call(merge_kernel, out_shape=jax.ShapeDtypeStruct(base.shape, B...]
where the time goes in v3:
time: 57.5 us; the launch traced here: 57.4 us
  Pallas kernels  57.4 us (100%)
    pallas_call x1, Pallas kernels, body(): pl.pallas_call(gather_kernel, out_shape=(jax.ShapeDtypeStruct((CHUNKS, 2,...  54.2 us
    pallas_call x1, Pallas kernels, body(): pl.pallas_call(merge_kernel, out_shape=jax.ShapeDtypeStruct(base.shape, B...  3.17 us

profile of v3, /device:TPU:1, one launch (start us, length us, event | category | flops | bytes accessed | tf_op | source)
XLA Modules:
  0.0 57.4 jit_solution(8995690374950358392)
XLA Ops:
  0.0 54.2 %gather_factors.1 = (bf16[2,2,8,64,1152]{4,3,2,1,0:T(8,128)(2,1)S(1)}, bf16[2,2,8,64,640]{4,3,2,1,0:T(8,128)(2,1)S(1)}, bf16[2,512,512]{2,1,0:T(8,128)(2,1)S(1)}, bf16[2,512,3584]{2,1,0:T(8,128)(2,1)S(1)}) custom-call(s32[8]{0:T(128)} %ranks_hbm.1, s32[8]{0:T(128)} %steps_hbm.1, s32[8]{0:T(128)} %slots_hbm.1, bf16[2,512,128]{2,1,0:T(8,128)(2,1)} %bitcast.3, ...), custom_call_target="tpu_custom_call" | custom-call | tf_op jit(solution)/shard_map/gather_factors/pallas_call | solution.py:488
  54.2 3.2 %merge_blocks.1 = bf16[2,512,3584]{2,1,0:T(8,128)(2,1)} custom-call(bf16[2,512,3584]{2,1,0:T(8,128)(2,1)S(1)} %get-tuple-element.9.work, bf16[2,512,512]{2,1,0:T(8,128)(2,1)S(1)} %get-tuple-element.10.packed_left, bf16[2,2,8,64,1152]{4,3,2,1,0:T(8,128)(2,1)S(1)} %get-tuple-element.11.r1, bf16[2,2,8,64,640]{4,3,2,1,0:T(8,128)(2,1)S(1)} %get-tuple-element.12.r2), custom_call_target="tpu_custom_call" | custom-call | tf_op jit(solution)/shard_map/merge_blocks/pallas_call | solution.py:517

commit v4 on v3

--- a/solution.py
+++ b/solution.py
@@ -13,15 +13,15 @@
 F32 = jnp.float32
 SLOTS = 8
 UNIT = 16
-DRAIN = 0
+DRAIN = 7
 CHUNKS = 2
-ROUTE1_TILES = 9
+ROUTE1_TILES = 8
 FIRST = (0, 1)
 PACED = {}
 SCHEDULE = (
-    "T0", "L1", "T1", "P0", "L0", "P1", "K0", "E0", "L3", "M0", "L2", "E1", "A0", "K1", "K2",
-    "K4", "M1", "L4", "L5", "K3", "Z0", "A1", "K5", "K6", "L6", "K7", "L7", "H0", "G0", "Z1",
-    "H1",
+    "T0", "L1", "T1", "P0", "P1", "L0", "K0", "E0", "L3", "M0", "E1", "L2", "A0", "L4", "K1",
+    "K2", "K4", "D2", "M1", "L5", "K3", "Z0", "A1", "K5", "K6", "L6", "K7", "L7", "H0", "I0",
+    "J0", "D4", "H1", "G0", "D2", "I1", "D1", "Z1", "J1",
 )
 
 
@@ -146,11 +146,12 @@
     over_z, sibling, over_zl = dev(zh_=zo), dev(core_=co), dev(zl_=zlo)
 
     barrier = pltpu.get_barrier_semaphore()
-    greeted = [right_x, left_x, over_z, sibling, over_zl, right_y, left_y, dev(y_=yo)]
+    greeted = []
     for a in range(2):
         for zh0 in range(2):
             for zl0 in range(2):
                 greeted.append(dev(x_=2 * zl + a, zh_=zh0, zl_=zl0))
+    greeted += [right_x, left_x, over_z, sibling, over_zl, right_y, left_y, dev(y_=yo)]
     for device in greeted:
         pl.semaphore_signal(barrier, inc=1, device_id=device, device_id_type=MESH)
 
@@ -226,7 +227,7 @@
     for c in FIRST:
         send_units(c)
     for c in range(CHUNKS):
-        if c not in FIRST:
+        if c not in FIRST and c in PACED.values():
             stage(c)
     L0 = N_A1 + N_A2
     own_left = lefts.at[col]
@@ -363,9 +364,9 @@
         got(r1, p, BLK[7], 16, HALF[1])
         share(p, 0, 7)
 
-    def shared(p):
-        for route in range(2):
-            for i in range(8):
+    def shared(p, blocks):
+        for i in blocks:
+            for route in range(2):
                 got((r1, r2)[route], p, BLK[i], 17 + route * 8 + i, half=co)
 
     def start_left():
@@ -403,7 +404,8 @@
         local[7].wait()
 
     steps_of = {
-        "T": turn, "P": pack, "E": early, "M": middle, "A": late, "Z": last, "H": shared, "G": merge,
+        "S": send_units, "T": turn, "P": pack, "E": early, "M": middle, "A": late, "Z": last, "H": lambda c: shared(c, (0, 4, 1, 2)), "I": lambda c: shared(c, (3, 5, 6)), "J": lambda c: shared(c, (7,)),
+        "D": lambda n: copies.drain(10 * n), "G": merge,
         "L": lambda n: (
             start_left,
             lambda: copies.start(own_left, own_left, L0 + 2, over_zl),

time: 57.5 us -> 56.6 us (0.984)
  Pallas kernels: 57.4 us -> 56.4 us
    pallas_call x1, Pallas kernels: 54.2 us -> 53.3 us  [body(): pl.pallas_call(gather_kernel, out_shape=(jax.ShapeDtypeStruct((CHUNKS, 2,...]
where the time goes in v4:
time: 56.6 us; the launch traced here: 56.5 us
  Pallas kernels  56.4 us (100%)
    pallas_call x1, Pallas kernels, body(): pl.pallas_call(gather_kernel, out_shape=(jax.ShapeDtypeStruct((CHUNKS, 2,...  53.3 us
    pallas_call x1, Pallas kernels, body(): pl.pallas_call(merge_kernel, out_shape=jax.ShapeDtypeStruct(base.shape, B...  3.2 us

profile of v4, /device:TPU:1, one launch (start us, length us, event | category | flops | bytes accessed | tf_op | source)
XLA Modules:
  0.0 56.5 jit_solution(17583526660959440893)
XLA Ops:
  0.0 53.3 %gather_factors.1 = (bf16[2,2,8,64,1024]{4,3,2,1,0:T(8,128)(2,1)S(1)}, bf16[2,2,8,64,768]{4,3,2,1,0:T(8,128)(2,1)S(1)}, bf16[2,512,512]{2,1,0:T(8,128)(2,1)S(1)}, bf16[2,512,3584]{2,1,0:T(8,128)(2,1)S(1)}) custom-call(s32[8]{0:T(128)} %ranks_hbm.1, s32[8]{0:T(128)} %steps_hbm.1, s32[8]{0:T(128)} %slots_hbm.1, bf16[2,512,128]{2,1,0:T(8,128)(2,1)} %bitcast.3, ...), custom_call_target="tpu_custom_call" | custom-call | tf_op jit(solution)/shard_map/gather_factors/pallas_call | solution.py:490
  53.3 3.2 %merge_blocks.1 = bf16[2,512,3584]{2,1,0:T(8,128)(2,1)} custom-call(bf16[2,512,3584]{2,1,0:T(8,128)(2,1)S(1)} %get-tuple-element.9.work, bf16[2,512,512]{2,1,0:T(8,128)(2,1)S(1)} %get-tuple-element.10.packed_left, bf16[2,2,8,64,1024]{4,3,2,1,0:T(8,128)(2,1)S(1)} %get-tuple-element.11.r1, bf16[2,2,8,64,768]{4,3,2,1,0:T(8,128)(2,1)S(1)} %get-tuple-element.12.r2), custom_call_target="tpu_custom_call" | custom-call | tf_op jit(solution)/shard_map/merge_blocks/pallas_call | solution.py:519

commit v5 on v4

--- a/solution.py
+++ b/solution.py
@@ -104,7 +104,7 @@
                 pl.when(when)(copy.wait_send)
 
 
-N_A1, N_A2, N_L, N_B = CHUNKS * 8, CHUNKS * 4, 9, 17 + 16
+N_A1, N_A2, N_L, N_B = CHUNKS * 8, CHUNKS * 4, 9, 17 + 8
 N_RECV = N_A1 + N_A2 + N_L + CHUNKS * N_B
 N_SEND = CHUNKS * (8 + 3 + N_B) + 9
 
@@ -116,8 +116,7 @@
     left,
     right_hbm,
     base,
-    r1,
-    r2,
+    r,
     packed_left,
     work,
     ranks,
@@ -283,91 +282,84 @@
     def b_event(p, n):
         return N_A1 + N_A2 + N_L + p * N_B + n
 
-    def at(ref, p, blk, rows=None, half=core):
-        return ref.at[p, half, blk] if rows is None else ref.at[p, half, blk, rows]
-
-    def go(ref, p, blk, n, device, rows=None):
-        copies.start(at(ref, p, blk, rows), at(ref, p, blk, rows), b_event(p, n), device)
-
-    def got(ref, p, blk, n, rows=None, half=core):
-        copies.arrived(at(ref, p, blk, rows, half), b_event(p, n), sibling)
-
-    def share(p, route, i):
-        go((r1, r2)[route], p, BLK[i], 17 + route * 8 + i, sibling)
+    r1 = pl.ds(0, ROUTE1_TILES * 128)
+    r2 = pl.ds(ROUTE1_TILES * 128, chunk_width - ROUTE1_TILES * 128)
+
+    def at(cols, p, blk, rows=None, half=core):
+        return r.at[p, half, blk, pl.ds(0, 64) if rows is None else rows, cols]
+
+    def go(cols, p, blk, n, device, rows=None):
+        copies.start(at(cols, p, blk, rows), at(cols, p, blk, rows), b_event(p, n), device)
+
+    def got(cols, p, blk, n, rows=None):
+        copies.arrived(at(cols, p, blk, rows), b_event(p, n), sibling)
+
+    def share(p, i):
+        block = r.at[p, core, BLK[i]]
+        copies.start(block, block, b_event(p, 17 + i), sibling)
 
     def pack(p):
         for y0 in (1, 2, 3):
             y2 = (y + y0) % 4
             copies.arrived(second[p].at[y2], a2_event(p, y2), sibling)
-        width = r1.shape[4]
         for i in range(4):
             slot, _ = slot_and_start(t + 8 * i, ends)
             unit = second[p][jnp.bitwise_and(slot, 3), jnp.right_shift(slot, 2)]
-            r1[p, core, t, pl.ds(UNIT * i, UNIT)] = unit[:, :width]
-            r2[p, core, t, pl.ds(UNIT * i, UNIT)] = unit[:, width:]
+            r[p, core, t, pl.ds(UNIT * i, UNIT)] = unit
         go(r2, p, t, 0, right_x)
         go(r2, p, t, 1, left_x)
         go(r1, p, t, 8, over_z)
         go(r1, p, t, 9, right_x)
         go(r1, p, t, 10, left_x)
         go(r2, p, t, 4, over_z)
-        share(p, 0, 0)
-        share(p, 1, 0)
+        share(p, 0)
 
     def early(p):
         got(r2, p, BLK[1], 0)
         go(r2, p, BLK[1], 2, right_x, HALF[0])
         go(r2, p, BLK[1], 5, over_z)
-        share(p, 1, 1)
         got(r2, p, BLK[2], 1)
         go(r2, p, BLK[2], 3, left_x, HALF[1])
         go(r2, p, BLK[2], 6, over_z)
-        share(p, 1, 2)
         got(r1, p, BLK[4], 8)
         go(r1, p, BLK[4], 13, right_x)
         go(r1, p, BLK[4], 14, left_x)
-        share(p, 0, 4)
 
     def middle(p):
         got(r1, p, BLK[1], 9)
         go(r1, p, BLK[1], 11, right_x, HALF[0])
-        share(p, 0, 1)
+        share(p, 1)
         got(r1, p, BLK[2], 10)
         go(r1, p, BLK[2], 12, left_x, HALF[1])
-        share(p, 0, 2)
+        share(p, 2)
         got(r2, p, BLK[3], 2, HALF[0])
         got(r2, p, BLK[3], 3, HALF[1])
         go(r2, p, BLK[3], 7, over_z)
-        share(p, 1, 3)
         got(r2, p, BLK[4], 4)
-        share(p, 1, 4)
+        share(p, 4)
 
     def late(p):
         got(r1, p, BLK[5], 13)
         go(r1, p, BLK[5], 15, right_x, HALF[0])
-        share(p, 0, 5)
         got(r1, p, BLK[6], 14)
         go(r1, p, BLK[6], 16, left_x, HALF[1])
-        share(p, 0, 6)
         got(r1, p, BLK[3], 11, HALF[0])
         got(r1, p, BLK[3], 12, HALF[1])
-        share(p, 0, 3)
+        share(p, 3)
         got(r2, p, BLK[5], 5)
-        share(p, 1, 5)
+        share(p, 5)
         got(r2, p, BLK[6], 6)
-        share(p, 1, 6)
+        share(p, 6)
 
     def last(p):
         got(r2, p, BLK[7], 7)
-        share(p, 1, 7)
         got(r1, p, BLK[7], 15, HALF[0])
         got(r1, p, BLK[7], 16, HALF[1])
-        share(p, 0, 7)
+        share(p, 7)
 
     def shared(p, blocks):
         for i in blocks:
-            for route in range(2):
-                got((r1, r2)[route], p, BLK[i], 17 + route * 8 + i, half=co)
+            copies.arrived(r.at[p, co, BLK[i]], b_event(p, 17 + i), sibling)
 
     def start_left():
         copies.start(own_left, own_left, L0 + 0, right_y)
@@ -388,8 +380,8 @@
         copies.start(lefts.at[c_r, 1], lefts.at[c_r, 1], L0 + 8, left_y)
 
     def merge(c):
-        for h, route, lo, hi in slices(r1.shape[4], r2.shape[4]):
-            merge_slice(c, h, route, lo, hi, work, packed_left, r1, r2)
+        for h, lo, hi in slices(chunk_width):
+            merge_slice(c, h, lo, hi, work, packed_left, r)
 
     def own_halves():
         copies.arrived(lefts.at[own_o, 0], L0 + 3, sibling)
@@ -430,21 +422,15 @@
     return chunk // per, (chunk % per) * width
 
 
-def slices(width1, width2, step=512):
-    cut = []
-    for h in range(2):
-        for route, width in enumerate((width1, width2)):
-            for lo in range(0, width, step):
-                cut.append((h, route, lo, min(lo + step, width)))
-    return cut
-
-
-def merge_slice(c, h, route, lo, hi, work, packed_left, r1, r2, out=None):
-    width1, half = r1.shape[4], work.shape[2] // 2
-    p, first = place(c, width1 + r2.shape[4])
-    begin = h * half + first + route * width1 + lo
+def slices(width, step=512):
+    return [(h, lo, min(lo + step, width)) for h in range(2) for lo in range(0, width, step)]
+
+
+def merge_slice(c, h, lo, hi, work, packed_left, r, out=None):
+    p, first = place(c, r.shape[4])
+    begin = h * (work.shape[2] // 2) + first + lo
     cols = slice(begin, begin + hi - lo)
-    rhs = (r1, r2)[route][c, h, :, :, lo:hi].reshape(packed_left.shape[2], hi - lo)
+    rhs = r[c, h, :, :, lo:hi].reshape(packed_left.shape[2], hi - lo)
     delta = jnp.dot(packed_left[p], rhs, preferred_element_type=F32)
     total = (work[p, :, cols].astype(F32) + delta).astype(BF16)
     if out is None:
@@ -454,9 +440,9 @@
     return p, cols
 
 
-def merge_kernel(work, packed_left, r1, r2, out, last, sems):
-    width1, width2, half = r1.shape[4], r2.shape[4], work.shape[2] // 2
-    p, lo = place(CHUNKS - 1, width1 + width2)
+def merge_kernel(work, packed_left, r, out, last, sems):
+    width, half = r.shape[4], work.shape[2] // 2
+    p, lo = place(CHUNKS - 1, width)
     pairs = [(work.at[p2], out.at[p2]) for p2 in range(p)]
     for h in range(2 if lo else 0):
         cols = slice(h * half, h * half + lo)
@@ -470,8 +456,8 @@
 
     for src, dst in pairs:
         send(src, dst)
-    for h, route, lo, hi in slices(width1, width2):
-        p, cols = merge_slice(CHUNKS - 1, h, route, lo, hi, work, packed_left, r1, r2, last)
+    for h, lo, hi in slices(width):
+        p, cols = merge_slice(CHUNKS - 1, h, lo, hi, work, packed_left, r, last)
         send(last.at[:, cols], out.at[p, :, cols])
     for copy in started:
         copy.wait()
@@ -483,20 +469,17 @@
     left = left.reshape(projections, rows, 128)
     right = right.reshape(projections, 8, UNIT, half)
     width = 2 * half // CHUNKS
-    w1 = ROUTE1_TILES * 128
-    w2 = width - w1
     vmem = pl.BlockSpec(memory_space=pltpu.VMEM)
     hbm = pl.BlockSpec(memory_space=pltpu.HBM)
-    r1, r2, packed_left, work = pl.pallas_call(
+    r, packed_left, work = pl.pallas_call(
         gather_kernel,
         out_shape=(
-            jax.ShapeDtypeStruct((CHUNKS, 2, 8, 64, w1), BF16),
-            jax.ShapeDtypeStruct((CHUNKS, 2, 8, 64, w2), BF16),
+            jax.ShapeDtypeStruct((CHUNKS, 2, 8, 64, width), BF16),
             jax.ShapeDtypeStruct((2, rows, 512), BF16),
             jax.ShapeDtypeStruct(base.shape, BF16),
         ),
         in_specs=[hbm] * 6,
-        out_specs=(vmem,) * 4,
+        out_specs=(vmem,) * 3,
         scratch_shapes=[
             pltpu.SMEM((SLOTS,), jnp.int32),
             pltpu.SMEM((SLOTS,), jnp.int32),
@@ -519,12 +502,12 @@
     return pl.pallas_call(
         merge_kernel,
         out_shape=jax.ShapeDtypeStruct(base.shape, BF16),
-        in_specs=[vmem] * 4,
+        in_specs=[vmem] * 3,
         out_specs=pl.BlockSpec(memory_space=pltpu.HBM),
         scratch_shapes=[pltpu.VMEM((rows, columns), BF16), pltpu.SemaphoreType.DMA((16,))],
         compiler_params=pltpu.CompilerParams(vmem_limit_bytes=24 * 2**20),
         name="merge_blocks",
-    )(work, packed_left, r1, r2)
+    )(work, packed_left, r)
 
 
 def solution(mesh):

time: 56.6 us -> 56.2 us (level)
  no operation moved by 1% of the time
where the time goes in v5:
time: 56.2 us; the launch traced here: 56.1 us
  Pallas kernels  56.1 us (100%)
    pallas_call x1, Pallas kernels, body(): pl.pallas_call(gather_kernel, out_shape=(jax.ShapeDtypeStruct((CHUNKS, 2,...  52.9 us
    pallas_call x1, Pallas kernels, body(): pl.pallas_call(merge_kernel, out_shape=jax.ShapeDtypeStruct(base.shape, B...  3.19 us

profile of v5, /device:TPU:1, one launch (start us, length us, event | category | flops | bytes accessed | tf_op | source)
XLA Modules:
  0.0 56.1 jit_solution(16335768663202754763)
XLA Ops:
  0.0 52.9 %gather_factors.1 = (bf16[2,2,8,64,1792]{4,3,2,1,0:T(8,128)(2,1)S(1)}, bf16[2,512,512]{2,1,0:T(8,128)(2,1)S(1)}, bf16[2,512,3584]{2,1,0:T(8,128)(2,1)S(1)}) custom-call(s32[8]{0:T(128)} %ranks_hbm.1, s32[8]{0:T(128)} %steps_hbm.1, s32[8]{0:T(128)} %slots_hbm.1, bf16[2,512,128]{2,1,0:T(8,128)(2,1)} %bitcast.3, bf16[2,8,16,1792]{3,2,1,0:T(8,128)(2,1)} %bitcast.2, ...), custom_call_target="tpu_custom_call" | custom-call | tf_op jit(solution)/shard_map/gather_factors/pallas_call | solution.py:474
  52.9 3.2 %merge_blocks.1 = bf16[2,512,3584]{2,1,0:T(8,128)(2,1)} custom-call(bf16[2,512,3584]{2,1,0:T(8,128)(2,1)S(1)} %get-tuple-element.8.work, bf16[2,512,512]{2,1,0:T(8,128)(2,1)S(1)} %get-tuple-element.9.packed_left, bf16[2,2,8,64,1792]{4,3,2,1,0:T(8,128)(2,1)S(1)} %get-tuple-element.10.r), custom_call_target="tpu_custom_call" | custom-call | tf_op jit(solution)/shard_map/merge_blocks/pallas_call | solution.py:502

commit v6 on v5

--- a/solution.py
+++ b/solution.py
@@ -21,7 +21,7 @@
 SCHEDULE = (
     "T0", "L1", "T1", "P0", "P1", "L0", "K0", "E0", "L3", "M0", "E1", "L2", "A0", "L4", "K1",
     "K2", "K4", "D2", "M1", "L5", "K3", "Z0", "A1", "K5", "K6", "L6", "K7", "L7", "H0", "I0",
-    "J0", "D4", "H1", "G0", "D2", "I1", "D1", "Z1", "J1",
+    "J0", "G0", "D3", "H1", "D1", "Z1", "I1", "J1",
 )
 
 

time: 56.2 us -> 56.2 us (level)
  no operation moved by 1% of the time
where the time goes in v6:
time: 56.2 us; the launch traced here: 56.1 us
  Pallas kernels  56.1 us (100%)
    pallas_call x1, Pallas kernels, body(): pl.pallas_call(gather_kernel, out_shape=(jax.ShapeDtypeStruct((CHUNKS, 2,...  52.9 us
    pallas_call x1, Pallas kernels, body(): pl.pallas_call(merge_kernel, out_shape=jax.ShapeDtypeStruct(base.shape, B...  3.19 us

profile of v6, /device:TPU:1, one launch (start us, length us, event | category | flops | bytes accessed | tf_op | source)
XLA Modules:
  0.0 56.1 jit_solution(11871201164024056182)
XLA Ops:
  0.0 52.9 %gather_factors.1 = (bf16[2,2,8,64,1792]{4,3,2,1,0:T(8,128)(2,1)S(1)}, bf16[2,512,512]{2,1,0:T(8,128)(2,1)S(1)}, bf16[2,512,3584]{2,1,0:T(8,128)(2,1)S(1)}) custom-call(s32[8]{0:T(128)} %ranks_hbm.1, s32[8]{0:T(128)} %steps_hbm.1, s32[8]{0:T(128)} %slots_hbm.1, bf16[2,512,128]{2,1,0:T(8,128)(2,1)} %bitcast.3, bf16[2,8,16,1792]{3,2,1,0:T(8,128)(2,1)} %bitcast.2, ...), custom_call_target="tpu_custom_call" | custom-call | tf_op jit(solution)/shard_map/gather_factors/pallas_call | solution.py:474
  52.9 3.2 %merge_blocks.1 = bf16[2,512,3584]{2,1,0:T(8,128)(2,1)} custom-call(bf16[2,512,3584]{2,1,0:T(8,128)(2,1)S(1)} %get-tuple-element.8.work, bf16[2,512,512]{2,1,0:T(8,128)(2,1)S(1)} %get-tuple-element.9.packed_left, bf16[2,2,8,64,1792]{4,3,2,1,0:T(8,128)(2,1)S(1)} %get-tuple-element.10.r), custom_call_target="tpu_custom_call" | custom-call | tf_op jit(solution)/shard_map/merge_blocks/pallas_call | solution.py:502
